TPU v7x, 32 devices: a whole 2x2x4 slice. The times are simulated.
32 devices in a mesh: sub: 8 (over y, x, core), rep: 4 (over z).
Axes of the slice: x: 2, y: 2, z: 4, core: 2. Of those that a mesh axis runs over, the one named last changes fastest.
Arguments:
- dual_ops: bfloat16 [32, 1024, 1024], P(('sub', 'rep'))
- mode_traces: float32 [32, 6, 1024], P(('sub', 'rep')), may hold values from -0.046875 to 0.046875
- route: int32 [32, 1024], P(('sub', 'rep')), may hold values from 0 to 1023, each once within a row
- mode_block: int32 [32, 1], replicated, may hold values from 0 to 1
- local_gap: float32 [32, 32768], P(None, ('sub', 'rep')), may hold values from -6 to 6
Outputs:
- multipliers: float32 [32, 32768], P(None, ('sub', 'rep'))
- amplitudes: float32 [32, 12], replicated
Inputs may be any that keep to these rules, and one draw needn't show every extreme that they name: Each row of route lists every number below 1024 once. `mode_block`: every aggregate holds at least one subdomain.
All inputs are finite; a program needn't handle non-finite values.
Results may differ from a plain program's by a relative error of at most 0.003.
Values sent between devices are 32-bit elements; how exact they have to be, the bound alone decides.
No kernel may reach another device: no remote copies, remote signals or barrier semaphores. Data moves between devices by JAX's collectives and lax.ppermute only.
A program may use at most 64 MiB of HBM per device.

v0:
```python
import functools

import jax
import jax.numpy as jnp
from jax import lax
from jax.experimental import pallas as pl
from jax.experimental.pallas import tpu as pltpu
from jax.sharding import PartitionSpec as P

MODES = 6
AGG_SUBS = 16
ITERS = 2
GROUP = 8

HIGHEST = lax.Precision.HIGHEST
VMEM = pl.BlockSpec(memory_space=pltpu.VMEM)
HBM = pl.BlockSpec(memory_space=pltpu.HBM)
NN = (((1,), (0,)), ((), ()))
NT = (((1,), (1,)), ((), ()))


def split(values):
    high = values.astype(jnp.bfloat16).astype(jnp.float32)
    return jnp.concatenate([high, values - high], axis=0).astype(jnp.bfloat16)


def split_dot(values, matrix, dims):
    rows = values.shape[0]
    both = lax.dot_general(split(values), matrix, dims, preferred_element_type=jnp.float32)
    return both[:rows] + both[rows:]


def small_dot(left, right):
    return jnp.dot(left, right, precision=HIGHEST, preferred_element_type=jnp.float32)


def send_far(values, far_ref, *pair_refs):
    height = values.shape[0]
    per_peer = pair_refs[0].shape[1]
    values = split(values)
    for at, ref in enumerate(pair_refs):
        columns = far_ref[:, 2 * at * per_peer : (2 * at + 2) * per_peer]
        slots = jnp.dot(values, columns, preferred_element_type=jnp.float32)
        slots = slots[:height] + slots[height:]
        ref[:height] = slots[:, :per_peer]
        ref[height:] = slots[:, per_peer:]


def send_near(values, edge_ref, near_ref, back_ref, stay_ref):
    per_peer = back_ref.shape[1]
    slots = split_dot(values, edge_ref[...], NN)
    for at, ref in enumerate((near_ref, back_ref, stay_ref)):
        ref[...] = slots[:, at * per_peer : (at + 1) * per_peer]


def straight(last_ref, pair_refs):
    height = last_ref.shape[0]
    return jnp.concatenate([*(ref[:height] for ref in pair_refs), last_ref[...]], axis=1)


def for_other(near_ref, pair_refs):
    height = near_ref.shape[0]
    return jnp.concatenate([near_ref[...], *(ref[height:] for ref in pair_refs)], axis=1)


def handed(got_ref, height, backwards=False):
    starts = list(range(height, got_ref.shape[0], height))
    starts = [0, *(starts[::-1] if backwards else starts)]
    return jnp.concatenate([got_ref[at : at + height] for at in starts], axis=1)


def spread(values, loads, groups):
    modes = values[loads:]
    label = modes[MODES : MODES + 1]
    used = lax.broadcasted_iota(jnp.int32, modes.shape, 0) < MODES
    parts = [jnp.where(used & (label == group), modes, 0.0) for group in range(groups)]
    return jnp.concatenate([values[:loads], *parts], axis=0)


def one_hot(route_ref, peer, per_peer):
    start = pl.multiple_of(peer * per_peer, per_peer)
    row_ids = lax.broadcasted_iota(jnp.int32, (route_ref.shape[1], per_peer), 0)
    return jnp.where(row_ids == route_ref[:, pl.ds(start, per_peer)], 1.0, 0.0).astype(jnp.bfloat16)


def place_kernel(
    route_hbm, block_hbm, gap_hbm, traces_hbm, operator_hbm,
    far_ref, values_ref, operator_ref, route_ref, *refs,
):
    *pair_refs, block_ref, traces_ref, sems = refs
    loads, rows = gap_hbm.shape
    per_peer = pair_refs[0].shape[1]
    peers = rows // per_peer
    copies = [
        pltpu.make_async_copy(source, target, sems.at[at])
        for at, (source, target) in enumerate(
            (
                (route_hbm, route_ref),
                (block_hbm, block_ref),
                (traces_hbm, traces_ref),
                (gap_hbm, values_ref.at[pl.ds(0, loads)]),
                (operator_hbm, operator_ref),
            )
        )
    ]

    def build(at):
        peer = own_index ^ (peers - 1 - at)
        far_ref[:, at * per_peer : (at + 1) * per_peer] = one_hot(route_ref, peer, per_peer)

    for copy in copies:
        copy.start()
    own_index = lax.axis_index("sub")
    device = own_index * lax.axis_size("rep") + lax.axis_index("rep")
    copies[0].wait()
    for at in range(peers - 4):
        build(at)
    copies[1].wait()
    copies[2].wait()
    blocks = block_ref[...]
    lane = lax.broadcasted_iota(jnp.int32, blocks.shape, 1)
    own_block = jnp.sum(jnp.where(lane == device, blocks, 0), axis=1, keepdims=True)
    modes = traces_ref.shape[0]
    label = jnp.broadcast_to(own_block.astype(jnp.float32), (1, rows))
    for mode in range(modes):
        values_ref[loads + mode : loads + mode + 1] = traces_ref[mode]
    values_ref[loads + modes : loads + modes + 1] = label
    values_ref[loads + modes + 1 :] = jnp.zeros((GROUP - modes - 1, rows), jnp.float32)
    copies[3].wait()
    for at in range(peers - 4, peers - 2):
        build(at)
    send_far(values_ref[...], far_ref, *pair_refs)
    copies[4].wait()


def ready_kernel(
    route_ref, far_ref, values_ref, operator_ref,
    edge_ref, slots_ref, placed_ref, near_ref, back_ref, stay_ref,
):
    per_peer = back_ref.shape[1]
    peers = far_ref.shape[1] // per_peer + 2
    own_index = lax.axis_index("sub")
    low = lax.broadcasted_iota(jnp.int32, (per_peer, per_peer), 0)
    high = lax.broadcasted_iota(jnp.int32, (per_peer, per_peer), 1)
    reverse = jnp.where(low + high == per_peer - 1, 1.0, 0.0).astype(jnp.bfloat16)
    own_columns = one_hot(route_ref, own_index, per_peer)
    near_columns = one_hot(route_ref, own_index ^ 1, per_peer)
    reversed_columns = jnp.dot(own_columns, reverse, preferred_element_type=jnp.float32).astype(jnp.bfloat16)
    edge_ref[...] = jnp.concatenate([near_columns, reversed_columns, own_columns], axis=1)
    for at in range(peers // 2 - 1):
        start = 2 * at * per_peer
        slots_ref[0, :, at * per_peer : (at + 1) * per_peer] = far_ref[:, start : start + per_peer]
        slots_ref[1, :, (at + 1) * per_peer : (at + 2) * per_peer] = far_ref[:, start + per_peer : start + 2 * per_peer]
    slots_ref[0, :, (peers // 2 - 1) * per_peer :] = own_columns
    slots_ref[1, :, :per_peer] = near_columns
    send_near(values_ref[...], edge_ref, near_ref, back_ref, stay_ref)
    operator = operator_ref[0]
    for half in range(2):
        placed_ref[half] = jnp.dot(
            operator, slots_ref[half], preferred_element_type=jnp.float32
        ).astype(operator.dtype)


def first_half_kernel(placed_ref, stay_ref, back_ref, *refs):
    *pair_refs, jump_ref, image_ref = refs
    sent_refs, got_refs = pair_refs[: len(pair_refs) // 2], pair_refs[len(pair_refs) // 2 :]
    loads = stay_ref.shape[0] - GROUP
    groups = (jump_ref.shape[0] - loads) // GROUP
    own, got = (spread(straight(*refs), loads, groups) for refs in ((stay_ref, sent_refs), (back_ref, got_refs)))
    jump_ref[...] = own - got
    image_ref[...] = split_dot(own - got, placed_ref[0], NT)


def first_kernel(far_ref, placed_ref, half_ref, got_ref, near_ref, *refs):
    sent_refs, (jump_ref, image_ref, *pair_refs) = refs[: len(refs) // 2 - 1], refs[len(refs) // 2 - 1 :]
    height = near_ref.shape[0]
    loads = height - GROUP
    groups = (image_ref.shape[0] - loads) // GROUP
    own, got = (spread(value, loads, groups) for value in (for_other(near_ref, sent_refs), handed(got_ref, height)))
    jump_ref[...] = own - got
    image = half_ref[...] + split_dot(own - got, placed_ref[1], NT)
    image_ref[...] = image
    send_far(image, far_ref, *pair_refs)


def products_of(left, right):
    rows, columns = left.shape[0], right.shape[0]
    both = lax.dot_general(split(left), split(right), NT, preferred_element_type=jnp.float32)
    both = both[:rows] + both[rows:]
    return both[:, :columns] + both[:, columns:]


def by_load(products):
    sums = [jnp.sum(product, axis=1, keepdims=True) for product in products]
    empty = [jnp.zeros_like(sums[0])] * (GROUP - len(sums))
    return jnp.concatenate(sums + empty, axis=1).T


def pack(by_mode, scalars, blocks):
    by_mode = by_mode + pltpu.roll(by_mode, by_mode.shape[1] // 2, 1)
    upper, lower = by_mode[:GROUP], by_mode[GROUP:]
    row = lax.broadcasted_iota(jnp.int32, upper.shape, 0)
    left = lax.broadcasted_iota(jnp.int32, upper.shape, 1) < upper.shape[1] // 2
    spare = [
        jnp.where(left, pltpu.roll(upper, 6, 0), pltpu.roll(upper, 4, 0)),
        jnp.where(left, pltpu.roll(upper, 2, 0), pltpu.roll(lower, 6, 0)),
        jnp.where(left, pltpu.roll(lower, 4, 0), pltpu.roll(lower, 2, 0)),
        jnp.where(row == MODES, *scalars),
    ]
    rows = jnp.concatenate(blocks, axis=0)
    parts = [jnp.where(row < MODES, rows[at * GROUP : (at + 1) * GROUP], spare[at]) for at in range(4)]
    return jnp.concatenate(parts, axis=0)


def unpack(terms):
    parts = [terms[at * GROUP : (at + 1) * GROUP] for at in range(4)]
    row = lax.broadcasted_iota(jnp.int32, parts[0].shape, 0)
    lane = lax.broadcasted_iota(jnp.int32, parts[0].shape, 1)
    half = terms.shape[1] // 2
    turned = [pltpu.roll(part, half, 1) for part in parts[:3]]
    upper = jnp.where(
        row < 2, pltpu.roll(parts[0], 2, 0), jnp.where(row < 4, pltpu.roll(turned[0], 4, 0), pltpu.roll(parts[1], 6, 0))
    )
    lower = jnp.where(
        row < 2, pltpu.roll(turned[1], 2, 0), jnp.where(row < 4, pltpu.roll(parts[2], 4, 0), pltpu.roll(turned[2], 6, 0))
    )
    by_mode = [jnp.where((row < MODES) & (lane < half), part, 0.0) for part in (upper, lower)]
    blocks = [jnp.where(row < MODES, part, 0.0) for part in parts]
    scalars = parts[3][MODES : MODES + 1], parts[3][MODES + 1 : MODES + 2]
    return jnp.concatenate(by_mode, axis=0), scalars, [jnp.concatenate(blocks[at : at + 2], axis=0) for at in (0, 2)]


def powers(coarse, loads):
    lane = lax.broadcasted_iota(jnp.int32, (coarse, 4 * loads), 1)
    row = lax.broadcasted_iota(jnp.int32, (coarse, 4 * loads), 0)

    def choose(at, *values):
        return functools.reduce(lambda rest, pair: jnp.where(at == pair[0], pair[1], rest), enumerate(values), 0.0 * lane)

    strip, group = lane // coarse, lane // loads
    by_mode = choose(strip, jnp.where(lane > row, 2.0, 0.0), 1.0, 3.0, 2.0)
    scalars = choose(group, 0.0, 1.0, 2.0, 3.0), choose(group, 2.0, 2.0)
    blocks = [choose(group, 0.0, 2.0, 2.0, 1.0), choose(group, 2.0, 3.0, 3.0, 1.0)]
    return pack(by_mode, [line[:1] for line in scalars], blocks)


def magnitude(operator_ref):
    tall = 2 * GROUP
    largest = jnp.zeros((tall, operator_ref.shape[2]), operator_ref.dtype)
    for start in range(0, operator_ref.shape[1], tall):
        part = operator_ref[0, start : start + tall]
        largest = jnp.maximum(largest, jnp.maximum(part, -part))
    largest = jnp.max(largest.astype(jnp.float32), axis=0, keepdims=True)
    return jnp.clip(jnp.max(largest, axis=1, keepdims=True), 1e-30, 1e30)


def scale_of(terms):
    last = terms[-GROUP:]
    half = last.shape[1] // 2
    lane = lax.broadcasted_iota(jnp.int32, last.shape, 1)
    return jnp.where(lane < half, pltpu.roll(last, half, 1), last)[GROUP - 1 :]


def middle_kernel(
    edge_ref, slots_ref, operator_ref, straight_ref, handed_ref, image_ref,
    basis_ref, scale_ref, powers_ref, terms_ref, sums_ref, near_ref, back_ref, stay_ref,
):
    image = image_ref[...]
    send_near(image, edge_ref, near_ref, back_ref, stay_ref)
    coarse = terms_ref.shape[0] // 3
    loads = image.shape[0] - coarse
    basis = split_dot(straight_ref[...], slots_ref[0], NT) + split_dot(handed_ref[...], slots_ref[1], NT)
    basis_ref[...] = basis
    scale = magnitude(operator_ref)
    scale_ref[...] = jnp.broadcast_to(scale, scale_ref.shape)
    image = image * (1.0 / scale)
    residual, residual_image = basis[:loads], image[:loads]
    lanes = terms_ref.shape[1]
    powers_ref[...] = powers(coarse, loads)
    empty = jnp.zeros((lanes - 2 * loads - 2 * coarse, basis.shape[1]), jnp.float32)
    both = products_of(
        jnp.concatenate([basis[loads:], image[loads:]]),
        jnp.concatenate([residual, basis[loads:], image[loads:], empty, residual_image]),
    )
    by_g, by_h = both[:coarse], both[coarse:]
    lane = lax.broadcasted_iota(jnp.int32, (coarse, lanes), 1)
    first, last = lane < loads, lane >= lanes - loads
    terms_ref[:coarse] = jnp.where(first | last, by_g, 0.0)
    terms_ref[coarse : 2 * coarse] = jnp.where(last, pltpu.roll(by_h, lanes - loads, 1), 0.0)
    row = lax.broadcasted_iota(jnp.int32, (coarse, lanes), 0)
    by_mode = jnp.where((lane <= row) | ((lane >= coarse) & (lane < 2 * coarse)), pltpu.roll(by_g, lanes - loads, 1), 0.0)
    terms_ref[2 * coarse :] = by_mode
    sums_ref[...] = by_load([residual * residual, residual * residual_image])


def second_half_kernel(slots_ref, placed_ref, scale_ref, stay_ref, back_ref, *refs):
    *pair_refs, jump_ref, second_ref = refs
    sent_refs, got_refs = pair_refs[: len(pair_refs) // 2], pair_refs[len(pair_refs) // 2 :]
    jump = straight(stay_ref, sent_refs) - straight(back_ref, got_refs)
    jump = jump * (1.0 / scale_ref[:1, : jump.shape[1]])
    jump_ref[...] = split_dot(jump, slots_ref[0], NT)
    second_ref[...] = split_dot(jump, placed_ref[0], NT)


def second_kernel(
    slots_ref, placed_ref, basis_ref, half_jump_ref, half_second_ref, scale_ref, early_ref, sums_ref, got_ref,
    near_ref, *refs,
):
    *sent_refs, jump_ref, terms_ref = refs
    coarse = terms_ref.shape[0] // 2
    loads = basis_ref.shape[0] - coarse
    jump = for_other(near_ref, sent_refs) - handed(got_ref, loads + coarse, backwards=True)
    inverse = 1.0 / scale_ref[:1]
    jump = jump * inverse[:, : jump.shape[1]]
    second = (half_second_ref[...] + split_dot(jump, placed_ref[1], NT)) * inverse
    jump = half_jump_ref[...] + split_dot(jump, slots_ref[1], NT)
    jump_ref[...] = jump
    basis = basis_ref[...]
    residual, jump_loads, second_loads = basis[:loads], jump[:loads], second[:loads]
    both = products_of(
        jnp.concatenate([basis[loads:], jump[loads:], second[loads:]]),
        jnp.concatenate([residual, jump_loads, second_loads, jump[loads:], second[loads:]]),
    )
    by_g, by_z, by_dz = (both[at * coarse : (at + 1) * coarse] for at in range(3))
    lanes = terms_ref.shape[1]
    lane = lax.broadcasted_iota(jnp.int32, (coarse, lanes), 1)
    group = lane // loads
    top = jnp.where(group == 1, by_z, jnp.where(group == 2, by_g, 0.0))
    low = jnp.where(group < 2, by_dz, jnp.where(group == 2, by_z, 0.0))
    row = lax.broadcasted_iota(jnp.int32, (coarse, lanes), 0)
    z_z = pltpu.roll(by_z, 2 * coarse, 1)
    strip = lane // coarse
    by_mode = jnp.where((lane > row) & (strip == 0), z_z, 0.0)
    by_mode = jnp.where(strip == 2, pltpu.roll(by_z, 3 * coarse, 1), by_mode)
    by_mode = jnp.where(strip == 3, pltpu.roll(by_g, 4 * coarse, 1), by_mode)
    diagonal = jnp.sum(jnp.where(lane == row, z_z, 0.0), axis=0, keepdims=True)
    sums = by_load([jump_loads * jump_loads, jump_loads * second_loads, residual * second_loads])
    scalars = (
        jnp.concatenate([sums_ref[0:1], sums_ref[1:2], sums[0:1], sums[1:2]], axis=1),
        jnp.concatenate([sums[2:3], diagonal[:, :loads], scale_ref[:1, : 2 * loads]], axis=1),
    )
    terms_ref[...] = pack(
        early_ref[2 * coarse :] + by_mode, scalars, [early_ref[:coarse] + top, early_ref[coarse : 2 * coarse] + low]
    )


def summed(refs, power):
    parts = [ref[...] for ref in reversed(refs)]
    scales = [scale_of(part) for part in parts]
    largest = functools.reduce(jnp.maximum, scales)
    inverse = 1.0 / largest
    for at, scale in enumerate(scales):
        factor = scale * inverse
        square = factor * factor
        high = jnp.where(power > 2, square * factor, square)
        parts[at] = parts[at] * jnp.where(power > 1, high, jnp.where(power > 0, factor, 1.0))
    while len(parts) > 1:
        parts = [low + high for low, high in zip(parts[::2], parts[1::2])]
    return parts[0], largest


def sum_kernel(count, powers_ref, *refs):
    power = powers_ref[...]
    total, scale = summed(refs[:count], power)
    row = lax.broadcasted_iota(jnp.int32, power.shape, 0)
    lane = lax.broadcasted_iota(jnp.int32, power.shape, 1)
    total = jnp.where((row == power.shape[0] - 1) & (lane >= power.shape[1] // 2), scale, total)
    for ref in refs[count:]:
        ref[...] = total


def eliminate(work, coarse):
    row = lax.broadcasted_iota(jnp.int32, work.shape, 0)
    for start in range(0, coarse, GROUP):
        pivots = range(start, start + MODES)
        columns = [jnp.broadcast_to(work[:, pivot : pivot + 1], work.shape) for pivot in pivots]
        square = [[column[pivot : pivot + 1] for column in columns] for pivot in pivots]
        rows = [work[pivot : pivot + 1] for pivot in pivots]
        for at in range(MODES):
            scale = 1.0 / square[at][at]
            rows[at] = rows[at] * scale
            square[at] = [value * scale for value in square[at]]
            for other in range(MODES):
                if other != at:
                    factor = square[other][at]
                    rows[other] = rows[other] - factor * rows[at]
                    square[other] = [
                        value if to <= at else value - factor * square[at][to]
                        for to, value in enumerate(square[other])
                    ]
        for column, solved in zip(columns, rows):
            work = work - column * solved
        for pivot, solved in zip(pivots, rows):
            work = jnp.where(row == pivot, solved, work)
    return work


def thin_dot(left, right):
    high, right_high = (value.astype(jnp.bfloat16).astype(jnp.float32) for value in (left, right))
    return jnp.dot(
        jnp.concatenate([high, left - high, high], axis=1).astype(jnp.bfloat16),
        jnp.concatenate([right_high, right_high, right - right_high], axis=0).astype(jnp.bfloat16),
        preferred_element_type=jnp.float32,
    )


def final_kernel(powers_ref, *refs):
    *parts_refs, basis_ref, jump_ref, scale_ref, multipliers_ref, amplitudes_ref = refs
    terms, scale = summed(parts_refs, powers_ref[...])
    coarse = terms.shape[0] // 2
    loads = basis_ref.shape[0] - coarse
    groups = coarse // GROUP

    def total(values):
        return jnp.sum(values, axis=0, keepdims=True)

    ratio = scale_ref[:1, : scale.shape[1]] / scale
    jump = jump_ref[...] * jnp.concatenate([ratio] * (jump_ref.shape[1] // ratio.shape[1]), axis=1)
    by_mode, (sums, last_sums), (top, low) = unpack(terms)
    res_res, res_image, jump_jump, jump_second = (sums[:, at * loads : (at + 1) * loads] for at in range(4))
    res_second, diagonal = last_sums[:, :loads], last_sums[:, loads : loads + coarse]
    coarse_res, jump_z, second_g, image_g = (top[:, at * loads : (at + 1) * loads] for at in range(4))
    res_dz, jump_dz, second_z, res_h = (low[:, at * loads : (at + 1) * loads] for at in range(4))
    triangles, g_h, z_dz, g_dz = (by_mode[:, at * coarse : (at + 1) * coarse] for at in range(4))
    row = lax.broadcasted_iota(jnp.int32, (coarse, coarse), 0)
    column = lax.broadcasted_iota(jnp.int32, (coarse, coarse), 1)
    unit = jnp.where(row == column, 1.0, 0.0)
    other = triangles.T
    gram = jnp.where(row >= column, triangles, other)
    z_z = jnp.where(row < column, triangles, jnp.where(row == column, diagonal, other))
    empty = jnp.zeros((coarse, 5 * coarse - 2 * loads), jnp.float32)
    solved = eliminate(
        jnp.concatenate([gram, g_h, coarse_res, image_g, unit, empty], axis=1), coarse
    )
    inverse_h = solved[:, coarse : 2 * coarse]
    amounts = solved[:, 2 * coarse : 2 * coarse + loads]
    inverse_image = solved[:, 2 * coarse + loads : 2 * coarse + 2 * loads]
    inverse = solved[:, 2 * coarse + 2 * loads : 3 * coarse + 2 * loads]
    products = small_dot(jnp.concatenate([inverse_h, g_h, z_z, g_dz, z_dz], axis=0), amounts)
    inverse_h_amounts, h_amounts, z_amounts, g_dz_amounts, z_dz_amounts = (
        products[at * coarse : (at + 1) * coarse] for at in range(5)
    )
    shares = 2.0 * (inverse_image - inverse_h_amounts)
    both = jnp.concatenate([amounts, shares], axis=0).T
    basis_g, jump_z_rows = basis_ref[loads:], jump[loads:]
    d = basis_ref[:loads] - thin_dot(both[:, :coarse], basis_g)
    u = jump[:loads] - thin_dot(both, jnp.concatenate([jump_z_rows, basis_g], axis=0))
    products = small_dot(jnp.concatenate([g_h, z_z], axis=0), shares)
    image_d = image_g - h_amounts
    inner = res_res - total(amounts * coarse_res)
    curvature = 2.0 * (res_image - total(amounts * (res_h + image_d)))
    u_u = jump_jump - total(amounts * (2.0 * jump_z - z_amounts) + 2.0 * image_d * shares)
    second_u = second_g - g_dz_amounts - products[:coarse]
    jump_u = second_z - z_dz_amounts - 0.5 * products[coarse:]
    d_second = res_second - total(amounts * (res_dz + second_u) + shares * res_h)
    u_second = jump_second - total(amounts * (jump_dz + jump_u) + shares * (0.5 * jump_z + second_u))
    step = inner / curvature
    renewed = step * step * u_u - inner
    grown = 1.0 + renewed / inner
    curvature = grown * grown * curvature - grown * step * (2.0 * d_second + u_u) + 2.0 * step * step * u_second
    second_step = renewed / curvature
    on_d, on_u = step + second_step * grown, second_step * step
    amplitudes = amounts - on_d * shares + 2.0 * on_u * small_dot(inverse, second_u)
    amplitudes_ref[...] = jnp.concatenate(
        [amplitudes[label * GROUP : label * GROUP + MODES] for label in range(groups)], axis=0
    )
    inverse = 1.0 / scale[:, :loads]
    weights = jnp.concatenate([on_d * inverse, on_u * inverse, jnp.zeros((6, loads), jnp.float32)], axis=0).T
    multipliers_ref[...] = weights[:, 0:1] * d - weights[:, 1:2] * u


def call(kernel, shapes, in_specs, name, scratch=(), flops=0):
    return pl.pallas_call(
        kernel,
        out_shape=[jax.ShapeDtypeStruct(*shape) for shape in shapes],
        in_specs=in_specs,
        out_specs=[VMEM] * len(shapes),
        scratch_shapes=scratch,
        compiler_params=pltpu.CompilerParams(vmem_limit_bytes=24 * 1024 * 1024),
        cost_estimate=pl.CostEstimate(flops=flops, bytes_accessed=2**20, transcendentals=0),
        name=name,
    )


def permute(values, offset, plane_offset=0):
    peers, planes = lax.axis_size("sub"), lax.axis_size("rep")
    offset = offset * planes + plane_offset
    return lax.ppermute(values, ("sub", "rep"), [(at, at ^ offset) for at in range(peers * planes)])


def to_chips(*pairs):
    return [permute(pair, 2 * (len(pairs) - at) + 1) for at, pair in enumerate(pairs)]


def to_core(near, *pairs):
    return permute(jnp.concatenate([near, *(pair[near.shape[0] :] for pair in pairs)], axis=0), 1)


def last_parts(terms, powers):
    chips = [(offset + 1, 0) for offset in reversed(range(2, lax.axis_size("sub"), 2))]
    planes = [(1, offset) for offset in reversed(range(1, lax.axis_size("rep")))]
    copies = [terms]
    for offsets, following in (([(1, 0)], len(chips)), (chips, len(planes))):
        parts = [permute(copy, *offset) for copy, offset in zip(copies, offsets)]
        kernel = functools.partial(sum_kernel, len(parts) + 1)
        copies = call(kernel, [(terms.shape, terms.dtype)] * following, [VMEM] * (len(parts) + 2), "sum")(
            powers, *parts, copies[0]
        )
    return [*(permute(copy, *offset) for copy, offset in zip(copies, planes)), copies[0]]


def fused_body(dual_ops, mode_traces, route, mode_block, local_gap):
    peers = lax.axis_size("sub")
    loads, rows = local_gap.shape
    modes = mode_traces.shape[1]
    subs = mode_block.shape[0]
    groups = subs // AGG_SUBS
    per_peer = rows // peers
    height = loads + GROUP * groups
    f32, i32 = jnp.float32, jnp.int32
    tall = ((height, rows), f32)
    wide = ((3 * GROUP * groups, 4 * loads), f32)

    def pairs(height):
        return [((2 * height, per_peer), f32)] * (peers // 2 - 1)

    def singles(height):
        return [((height, per_peer), f32)] * 3

    def held(value):
        return pltpu.with_memory_space_constraint(value, pltpu.HBM)

    inputs = [route, mode_block.reshape(1, subs), local_gap, mode_traces.transpose(1, 0, 2), dual_ops]
    short = loads + GROUP
    far, values, operator, route, *send = call(
        place_kernel,
        [
            ((rows, rows - 2 * per_peer), jnp.bfloat16),
            ((short, rows), f32),
            (dual_ops.shape, dual_ops.dtype),
            (route.shape, i32),
            *pairs(short),
        ],
        [HBM] * 5,
        "place",
        [pltpu.VMEM((1, subs), i32), pltpu.VMEM((modes, 1, rows), f32), pltpu.SemaphoreType.DMA((5,))],
    )(*(held(value) for value in inputs))
    got = to_chips(*send)
    halves = ((2, rows, rows // 2), dual_ops.dtype)
    edge, slots, placed, near, back, stay = call(
        ready_kernel,
        [((rows, 3 * per_peer), jnp.bfloat16), halves, halves, *singles(short)],
        [VMEM] * 4,
        "ready",
        flops=2 * rows * rows * rows,
    )(route, far, values, operator)
    got_near = to_core(near, *got)
    half = ((height, rows // 2), f32)
    straight_jump, half_image = call(
        first_half_kernel, [half, tall], [VMEM] * (3 + 2 * len(got)), "first_half", flops=2 * rows * rows * height
    )(placed, stay, back, *send, *got)
    handed_jump, image, *image_send = call(
        first_kernel, [half, tall, *pairs(height)], [VMEM] * (5 + len(send)), "first"
    )(far, placed, half_image, got_near, near, *send)
    got = to_chips(*image_send)
    packed = ((2 * GROUP * groups, 4 * loads), f32)
    basis, scale, powers, terms, sums, near, back, stay = call(
        middle_kernel,
        [tall, ((GROUP, rows), f32), packed, wide, ((GROUP, loads), f32), *singles(height)],
        [VMEM] * 6,
        "middle",
        flops=4 * rows * rows * height,
    )(edge, slots, operator, straight_jump, handed_jump, image)
    got_near = to_core(near, *got[::-1])
    half_jump, half_second = call(
        second_half_kernel, [tall, tall], [VMEM] * (5 + 2 * len(got)), "second_half", flops=4 * rows * rows * height
    )(slots, placed, scale, stay, back, *image_send, *got)
    jump, terms = call(second_kernel, [tall, packed], [VMEM] * (10 + len(got)), "second")(
        slots, placed, basis, half_jump, half_second, scale, terms, sums, got_near, near, *image_send
    )
    parts = last_parts(terms, powers)
    multipliers, amplitudes = call(
        final_kernel, [((loads, rows), f32), ((MODES * groups, loads), f32)], [VMEM] * (4 + len(parts)), "final"
    )(powers, *parts, basis, jump, scale)
    return multipliers, amplitudes.T


def general_body(dual_ops, mode_traces, route, mode_block, local_gap):
    own_index = lax.axis_index("sub")
    plane_index = lax.axis_index("rep")
    peer_count = lax.axis_size("sub")
    plane_count = lax.axis_size("rep")
    operator = dual_ops[0]
    traces = mode_traces[0]
    slot_rows = route[0]
    rows_here = operator.shape[0]
    load_cases = local_gap.shape[0]
    per_peer = rows_here // peer_count
    blocks = mode_block[:, 0]
    block_count = blocks.shape[0] // AGG_SUBS
    coarse = block_count * MODES
    positions = jnp.arange(rows_here, dtype=jnp.int32)
    inverse = jnp.zeros((rows_here,), jnp.int32).at[slot_rows].set(positions)
    slot_peer = positions // per_peer
    within = positions % per_peer
    flip_index = jnp.where(
        slot_peer == own_index, slot_peer * per_peer + per_peer - 1 - within, positions
    )
    peer_ids = jnp.arange(peer_count, dtype=jnp.int32)
    peer_blocks = blocks[peer_ids * plane_count + plane_index]
    own_block = blocks[own_index * plane_count + plane_index]
    labels = jnp.arange(block_count, dtype=jnp.int32)
    peer_onehot = (peer_blocks[:, None] == labels[None, :]).astype(jnp.float32)
    own_onehot = (labels == own_block).astype(jnp.float32)
    trace_slots = traces[:, slot_rows]
    receive_index = flip_index[inverse]

    def to_peers(values):
        return values[:, slot_rows]

    def from_peers(values):
        return values[:, inverse]

    gap_peers = to_peers(local_gap)
    got_traces = lax.all_to_all(trace_slots, "sub", split_axis=1, concat_axis=1, tiled=True)
    got_gap = lax.all_to_all(gap_peers, "sub", split_axis=1, concat_axis=1, tiled=True)
    partner_traces = got_traces[:, flip_index]
    residual = local_gap - got_gap[:, receive_index]
    own_gram = jnp.dot(traces, traces.T, precision=HIGHEST)
    paired = (trace_slots[:, None, :] * partner_traces[None, :, :]).reshape(
        MODES, MODES, peer_count, per_peer
    )
    cross_terms = jnp.sum(paired, axis=3)
    cross_blocks = jnp.einsum("klq,qb->kbl", cross_terms, peer_onehot, precision=HIGHEST)
    own_blocks = own_gram[:, None, :] * own_onehot[None, :, None]
    row_term = 2.0 * (own_blocks - cross_blocks).reshape(MODES, coarse)
    gram_term = (own_onehot[:, None, None] * row_term[None]).reshape(coarse, coarse)

    def coarse_term(values):
        own_part = 2.0 * jnp.dot(values, traces.T, precision=HIGHEST)
        return (own_part[:, None, :] * own_onehot[None, :, None]).reshape(load_cases, coarse)

    def expand(amounts):
        grouped = amounts.reshape(load_cases, block_count, MODES)
        own_amounts = lax.dynamic_index_in_dim(grouped, own_block, 1, keepdims=False)
        own_part = jnp.dot(own_amounts, traces, precision=HIGHEST)
        peer_amounts = jnp.einsum("qb,rbk->rkq", peer_onehot, grouped, precision=HIGHEST)
        spread = jnp.repeat(peer_amounts, per_peer, axis=2)
        peer_part = jnp.sum(spread * partner_traces[None, :, :], axis=1)
        return own_part - from_peers(peer_part)

    squares = jnp.sum(residual * residual, axis=1)
    gram_matrix, coarse_res, norm_res = lax.psum(
        (gram_term, coarse_term(residual), squares), ("sub", "rep")
    )
    factor = jnp.linalg.cholesky(gram_matrix)

    def solve_coarse(right):
        return jax.scipy.linalg.cho_solve((factor, True), right.T).T

    amplitudes = solve_coarse(coarse_res)
    projected = residual - expand(amplitudes)
    inner_sum = norm_res - jnp.sum(amplitudes * coarse_res, axis=1)
    direction = projected
    multipliers = jnp.zeros_like(residual)
    for iteration in range(ITERS):
        product = lax.dot_general(
            direction.astype(jnp.bfloat16),
            operator,
            (((1,), (1,)), ((), ())),
            preferred_element_type=jnp.float32,
        )
        got_product = lax.all_to_all(
            to_peers(product), "sub", split_axis=1, concat_axis=1, tiled=True
        )
        image_jump = product - got_product[:, receive_index]
        coarse_jump, jump_squares, residual_cross, curvature = lax.psum(
            (
                coarse_term(image_jump),
                jnp.sum(image_jump * image_jump, axis=1),
                jnp.sum(residual * image_jump, axis=1),
                jnp.sum(direction * image_jump, axis=1),
            ),
            ("sub", "rep"),
        )
        step_size = inner_sum / curvature
        multipliers = multipliers + step_size[:, None] * direction
        residual = residual - step_size[:, None] * image_jump
        coarse_res = coarse_res - step_size[:, None] * coarse_jump
        norm_res = (
            norm_res - 2.0 * step_size * residual_cross + step_size * step_size * jump_squares
        )
        amplitudes = solve_coarse(coarse_res)
        if iteration + 1 < ITERS:
            projected = residual - expand(amplitudes)
            renewed = norm_res - jnp.sum(amplitudes * coarse_res, axis=1)
            direction = projected + (renewed / inner_sum)[:, None] * direction
            inner_sum = renewed
    return (multipliers, amplitudes)


def fits(mesh, dual_ops, mode_block, local_gap):
    peers, planes = mesh.shape["sub"], mesh.shape["rep"]
    powers = all(size & (size - 1) == 0 for size in (peers, planes))
    whole = dual_ops.shape[1] % (128 * peers) == 0 and local_gap.shape[0] % 16 == 0
    coarse = GROUP * (mode_block.shape[0] // AGG_SUBS)
    return powers and whole and 4 * local_gap.shape[0] == 128 and 8 * coarse == 128


def solution(mesh):
    placed = (
        P(("sub", "rep"), None, None),
        P(("sub", "rep"), None, None),
        P(("sub", "rep"), None),
        P(),
        P(None, ("sub", "rep")),
    )

    def run(dual_ops, mode_traces, route, mode_block, local_gap):
        body = fused_body if fits(mesh, dual_ops, mode_block, local_gap) else general_body
        return jax.shard_map(
            body, mesh=mesh, in_specs=placed, out_specs=(P(None, ("sub", "rep")), P()), check_vma=False
        )(dual_ops, mode_traces, route, mode_block, local_gap)

    return run
```

profile of v0, /device:TPU:0, one launch (start us, length us, event | category | flops | bytes accessed | tf_op | source)
XLA Modules:
  0.0 38.1 jit_solution(5249980303953056054)
XLA Ops:
  0.6 1.8 %place.1 = (bf16[1024,768]{1,0:T(8,128)(2,1)S(1)}, f32[40,1024]{1,0:T(8,128)S(1)}, bf16[1,1024,1024]{2,1,0:T(8,128)(2,1)S(1)}, s32[1,1024]{1,0:T(1,128)S(1)}, f3...) custom-call(s32[1,1024]{1,0:T(1,128)} %route_hbm.1, s32[1,32]{1,0:T(1,128)} %bitcast.4, ...), custom_call_target="tpu_custom_call" | custom-call | bytes 1048576 | tf_op jit(solution)/shard_map/place/pallas_call | solution.py:535
  2.4 3.4 %collective-permute-start = (f32[80,128]{1,0:T(8,128)S(1)}, f32[80,128]{1,0:T(8,128)S(1)}, u32[]{:S(2)}, u32[]{:S(2)}) collective-permute-start(f32[80,128]{1,0:T(8,128)S(1)} %get-tuple-element.51.refs_0_), channel_id=1, source_target_pairs={{0,28},{1,29},{2,30},{3,31},{4,24},{5,25},{6,26},{7,27},{8,20},{9,... | collective-permute-start | bytes 122888 | tf_op jit(solution)/shard_map/ppermute | solution.py:488
  5.8 0.8 %collective-permute-start.1 = (f32[80,128]{1,0:T(8,128)S(1)}, f32[80,128]{1,0:T(8,128)S(1)}, u32[]{:S(2)}, u32[]{:S(2)}) collective-permute-start(f32[80,128]{1,0:T(8,128)S(1)} %get-tuple-element.52.refs_1_), channel_id=1, source_target_pairs={{0,20},{1,21},{2,22},{3,23},{4,16},{5,17},{6,18},{7,19},{8,28},{9,... | collective-permute-start | bytes 122888 | tf_op jit(solution)/shard_map/ppermute | solution.py:488
  6.6 0.1 collective-permute-start.2
  6.7 3.0 %ready.1 = (bf16[1024,384]{1,0:T(8,128)(2,1)S(1)}, bf16[2,1024,512]{2,1,0:T(8,128)(2,1)S(1)}, bf16[2,1024,512]{2,1,0:T(8,128)(2,1)S(1)}, f32[40,128]{1,0:T(8,128...) custom-call(s32[1,1024]{1,0:T(1,128)S(1)} %get-tuple-element.42.route_ref, ...), custom_call_target="tpu_custom_call" | custom-call | flops 2147483648 | bytes 1048576 | tf_op jit(solution)/shard_map/ready/pallas_call | solution.py:550
  9.7 0.7 %collective-permute-done.2.refs_5_ = f32[80,128]{1,0:T(8,128)S(1)} collective-permute-done((f32[80,128]{1,0:T(8,128)S(1)}, f32[80,128]{1,0:T(8,128)S(1)}, u32[]{:S(2)}, u32[]{:S(2)}) %collective-permute-start.2) | collective-permute-done | bytes 40992 | tf_op jit(solution)/shard_map/ppermute | solution.py:488
  10.4 0.0 collective-permute-done.1.refs_4_
  10.4 0.0 collective-permute-done.refs_3_
  10.4 0.2 collective-permute-start.3
  10.6 0.4 %first_half.1 = (f32[48,512]{1,0:T(8,128)S(1)}, f32[48,1024]{1,0:T(8,128)S(1)}) custom-call(bf16[2,1024,512]{2,1,0:T(8,128)(2,1)S(1)} %get-tuple-element.48.placed_ref, f32[40,128]{1,0:T(8,128)S(1)} %get-tuple-element.49.stay_ref, f32[40,128]{1,0:T(8,128)S(1)} %get-tuple-element.50.back_ref, f32[80,128]{1,0:T(8,128)S(1)} %get-tuple-element.51.refs_0_, ...), custom_call_target="tpu_custom_call" | custom-call | flops 100663296 | bytes 1048576 | tf_op jit(solution)/shard_map/first_half/pallas_call | solution.py:559
  11.1 0.7 %collective-permute-done.3.got_ref = f32[160,128]{1,0:T(8,128)S(1)} collective-permute-done((f32[160,128]{1,0:T(8,128)S(1)}, f32[160,128]{1,0:T(8,128)S(1)}, u32[]{:S(2)}, u32[]{:S(2)}) %collective-permute-start.3) | collective-permute-done | bytes 81952 | tf_op jit(solution)/shard_map/ppermute | solution.py:488
  11.8 0.8 %first.1 = (f32[48,512]{1,0:T(8,128)S(1)}, f32[48,1024]{1,0:T(8,128)S(1)}, f32[96,128]{1,0:T(8,128)S(1)}, f32[96,128]{1,0:T(8,128)S(1)}, f32[96,128]{1,0:T(8,128)S(1)}) custom-call(bf16[1024,768]{1,0:T(8,128)(2,1)S(1)} %get-tuple-element.43.far_ref, bf16[2,1024,512]{2,1,0:T(8,128)(2,1)S(1)} %get-tuple-element.48.placed_ref, ...), custom_call_target="tpu_custom_call" | custom-call | bytes 1048576 | tf_op jit(solution)/shard_map/first/pallas_call | solution.py:562
  12.6 1.9 %collective-permute-start.4 = (f32[96,128]{1,0:T(8,128)S(1)}, f32[96,128]{1,0:T(8,128)S(1)}, u32[]{:S(2)}, u32[]{:S(2)}) collective-permute-start(f32[96,128]{1,0:T(8,128)S(1)} %get-tuple-element.64.refs_0_), channel_id=1, source_target_pairs={{0,28},{1,29},{2,30},{3,31},{4,24},{5,25},{6,26},{7,27},{8,20},{9,... | collective-permute-start | bytes 147464 | tf_op jit(solution)/shard_map/ppermute | solution.py:488
  14.5 0.3 collective-permute-start.5
  14.8 0.8 %collective-permute-start.6 = (f32[96,128]{1,0:T(8,128)S(1)}, f32[96,128]{1,0:T(8,128)S(1)}, u32[]{:S(2)}, u32[]{:S(2)}) collective-permute-start(f32[96,128]{1,0:T(8,128)S(1)} %get-tuple-element.66.refs_2_), channel_id=1, source_target_pairs={{0,12},{1,13},{2,14},{3,15},{4,8},{5,9},{6,10},{7,11},{8,4},{9,5},... | collective-permute-start | bytes 147464 | tf_op jit(solution)/shard_map/ppermute | solution.py:488
  15.6 1.3 %middle.1 = (f32[48,1024]{1,0:T(8,128)S(1)}, f32[8,1024]{1,0:T(8,128)S(1)}, f32[32,128]{1,0:T(8,128)S(1)}, f32[48,128]{1,0:T(8,128)S(1)}, f32[8,32]{1,0:T(8,128)...) custom-call(bf16[1024,384]{1,0:T(8,128)(2,1)S(1)} %get-tuple-element.46.edge_ref, ...), custom_call_target="tpu_custom_call" | custom-call | flops 201326592 | bytes 1048576 | tf_op jit(solution)/shard_map/middle/pallas_call | solution.py:567
  16.9 0.3 collective-permute-done.4.refs_3_
  17.2 1.1 %collective-permute-done.5.refs_4_ = f32[96,128]{1,0:T(8,128)S(1)} collective-permute-done((f32[96,128]{1,0:T(8,128)S(1)}, f32[96,128]{1,0:T(8,128)S(1)}, u32[]{:S(2)}, u32[]{:S(2)}) %collective-permute-start.5) | collective-permute-done | bytes 49184 | tf_op jit(solution)/shard_map/ppermute | solution.py:488
  18.3 0.0 collective-permute-done.6.refs_5_
  18.3 0.4 %collective-permute-start.7 = (f32[192,128]{1,0:T(8,128)S(1)}, f32[192,128]{1,0:T(8,128)S(1)}, u32[]{:S(2)}, u32[]{:S(2)}) collective-permute-start(f32[192,128]{1,0:T(8,128)S(1)} %pad_maximum_fusion), channel_id=1, source_target_pairs={{0,4},{1,5},{2,6},{3,7},{4,0},{5,1},{6,2},{7,3},{8,12},{9,13},{10,... | collective-permute-start | bytes 294920 | tf_op jit(solution)/shard_map/ppermute | solution.py:488
  18.7 0.7 %second_half.1 = (f32[48,1024]{1,0:T(8,128)S(1)}, f32[48,1024]{1,0:T(8,128)S(1)}) custom-call(bf16[2,1024,512]{2,1,0:T(8,128)(2,1)S(1)} %get-tuple-element.47.slots_ref, bf16[2,1024,512]{2,1,0:T(8,128)(2,1)S(1)} %get-tuple-element.48.placed_ref, f32[8,1024]{1,0:T(8,128)S(1)} %get-tuple-element.61.scale_ref.refs_6_, ...), custom_call_target="tpu_custom_call" | custom-call | flops 201326592 | bytes 1048576 | tf_op jit(solution)/shard_map/second_half/pallas_call | solution.py:575
  19.5 0.2 collective-permute-done.7.got_ref
  19.7 1.3 %second.1 = (f32[48,1024]{1,0:T(8,128)S(1)}, f32[32,128]{1,0:T(8,128)S(1)}) custom-call(bf16[2,1024,512]{2,1,0:T(8,128)(2,1)S(1)} %get-tuple-element.47.slots_ref, bf16[2,1024,512]{2,1,0:T(8,128)(2,1)S(1)} %get-tuple-element.48.placed_ref, f32[48,1024]{1,0:T(8,128)S(1)} %get-tuple-element.60.basis_ref.refs_4_, ...), custom_call_target="tpu_custom_call" | custom-call | bytes 1048576 | tf_op jit(solution)/shard_map/second/pallas_call | solution.py:578
  20.9 0.4 %collective-permute-start.8 = (f32[32,128]{1,0:T(8,128)S(1)}, f32[32,128]{1,0:T(8,128)S(1)}, u32[]{:S(2)}, u32[]{:S(2)}) collective-permute-start(f32[32,128]{1,0:T(8,128)S(1)} %get-tuple-element.72.refs_1_), channel_id=1, source_target_pairs={{0,4},{1,5},{2,6},{3,7},{4,0},{5,1},{6,2},{7,3},{8,12},{9,13},{10,... | collective-permute-start | bytes 49160 | tf_op jit(solution)/shard_map/ppermute | solution.py:488
  21.3 0.8 %collective-permute-done.8.refs_0_ = f32[32,128]{1,0:T(8,128)S(1)} collective-permute-done((f32[32,128]{1,0:T(8,128)S(1)}, f32[32,128]{1,0:T(8,128)S(1)}, u32[]{:S(2)}, u32[]{:S(2)}) %collective-permute-start.8) | collective-permute-done | bytes 16416 | tf_op jit(solution)/shard_map/ppermute | solution.py:488
  22.2 0.1 sum.2
  22.3 2.0 %collective-permute-start.9 = (f32[32,128]{1,0:T(8,128)S(1)}, f32[32,128]{1,0:T(8,128)S(1)}, u32[]{:S(2)}, u32[]{:S(2)}) collective-permute-start(f32[32,128]{1,0:T(8,128)S(1)} %get-tuple-element.73.refs_3_), channel_id=1, source_target_pairs={{0,28},{1,29},{2,30},{3,31},{4,24},{5,25},{6,26},{7,27},{8,20},{9,... | collective-permute-start | bytes 49160 | tf_op jit(solution)/shard_map/ppermute | solution.py:488
  24.3 0.4 %collective-permute-start.10 = (f32[32,128]{1,0:T(8,128)S(1)}, f32[32,128]{1,0:T(8,128)S(1)}, u32[]{:S(2)}, u32[]{:S(2)}) collective-permute-start(f32[32,128]{1,0:T(8,128)S(1)} %get-tuple-element.74), channel_id=1, source_target_pairs={{0,20},{1,21},{2,22},{3,23},{4,16},{5,17},{6,18},{7,19},{8,28},{9,... | collective-permute-start | bytes 49160 | tf_op jit(solution)/shard_map/ppermute | solution.py:488
  24.7 0.8 %collective-permute-start.11 = (f32[32,128]{1,0:T(8,128)S(1)}, f32[32,128]{1,0:T(8,128)S(1)}, u32[]{:S(2)}, u32[]{:S(2)}) collective-permute-start(f32[32,128]{1,0:T(8,128)S(1)} %get-tuple-element.75), channel_id=1, source_target_pairs={{0,12},{1,13},{2,14},{3,15},{4,8},{5,9},{6,10},{7,11},{8,4},{9,5},... | collective-permute-start | bytes 49160 | tf_op jit(solution)/shard_map/ppermute | solution.py:488
  25.5 0.9 %collective-permute-done.9.refs_0_ = f32[32,128]{1,0:T(8,128)S(1)} collective-permute-done((f32[32,128]{1,0:T(8,128)S(1)}, f32[32,128]{1,0:T(8,128)S(1)}, u32[]{:S(2)}, u32[]{:S(2)}) %collective-permute-start.9) | collective-permute-done | bytes 16416 | tf_op jit(solution)/shard_map/ppermute | solution.py:488
  26.4 1.1 %collective-permute-done.10.refs_1_ = f32[32,128]{1,0:T(8,128)S(1)} collective-permute-done((f32[32,128]{1,0:T(8,128)S(1)}, f32[32,128]{1,0:T(8,128)S(1)}, u32[]{:S(2)}, u32[]{:S(2)}) %collective-permute-start.10) | collective-permute-done | bytes 16416 | tf_op jit(solution)/shard_map/ppermute | solution.py:488
  27.5 0.4 %collective-permute-done.11.refs_2_ = f32[32,128]{1,0:T(8,128)S(1)} collective-permute-done((f32[32,128]{1,0:T(8,128)S(1)}, f32[32,128]{1,0:T(8,128)S(1)}, u32[]{:S(2)}, u32[]{:S(2)}) %collective-permute-start.11) | collective-permute-done | bytes 16416 | tf_op jit(solution)/shard_map/ppermute | solution.py:488
  27.9 0.1 sum.3
  28.0 3.4 %collective-permute-start.12 = (f32[32,128]{1,0:T(8,128)S(1)}, f32[32,128]{1,0:T(8,128)S(1)}, u32[]{:S(2)}, u32[]{:S(2)}) collective-permute-start(f32[32,128]{1,0:T(8,128)S(1)} %get-tuple-element.76.refs_3_), channel_id=1, source_target_pairs={{0,7},{1,6},{2,5},{3,4},{4,3},{5,2},{6,1},{7,0},{8,15},{9,14},{10,... | collective-permute-start | bytes 49160 | tf_op jit(solution)/shard_map/ppermute | solution.py:488
  31.4 0.0 collective-permute-start.13
  31.4 0.6 %collective-permute-start.14 = (f32[32,128]{1,0:T(8,128)S(1)}, f32[32,128]{1,0:T(8,128)S(1)}, u32[]{:S(2)}, u32[]{:S(2)}) collective-permute-start(f32[32,128]{1,0:T(8,128)S(1)} %get-tuple-element.78), channel_id=1, source_target_pairs={{0,5},{1,4},{2,7},{3,6},{4,1},{5,0},{6,3},{7,2},{8,13},{9,12},{10,... | collective-permute-start | bytes 49160 | tf_op jit(solution)/shard_map/ppermute | solution.py:488
  32.0 1.0 %collective-permute-done.12.refs_0_ = f32[32,128]{1,0:T(8,128)S(1)} collective-permute-done((f32[32,128]{1,0:T(8,128)S(1)}, f32[32,128]{1,0:T(8,128)S(1)}, u32[]{:S(2)}, u32[]{:S(2)}) %collective-permute-start.12) | collective-permute-done | bytes 16416 | tf_op jit(solution)/shard_map/ppermute | solution.py:488
  33.0 2.5 %collective-permute-done.13.refs_1_ = f32[32,128]{1,0:T(8,128)S(1)} collective-permute-done((f32[32,128]{1,0:T(8,128)S(1)}, f32[32,128]{1,0:T(8,128)S(1)}, u32[]{:S(2)}, u32[]{:S(2)}) %collective-permute-start.13) | collective-permute-done | bytes 16416 | tf_op jit(solution)/shard_map/ppermute | solution.py:488
  35.5 0.0 collective-permute-done.14.refs_2_
  35.5 2.6 %final.1 = (f32[32,1024]{1,0:T(8,128)}, f32[12,32]{1,0:T(8,128)}) custom-call(f32[32,128]{1,0:T(8,128)S(1)} %get-tuple-element.59.powers_ref, f32[32,128]{1,0:T(8,128)S(1)} %collective-permute-done.12.refs_0_, f32[32,128]{1,0:T(8,128)S(1)} %collective-permute-done.13.refs_1_, f32[32,128]{1,0:T(8,128)S(1)} %collective-permute-done.14.refs_2_, ...), custom_call_target="tpu_custom_call" | custom-call | bytes 1048576 | tf_op jit(solution)/shard_map/final/pallas_call | solution.py:582
  (8 shorter events, 0.0 us)
Async XLA Ops:
  2.4 8.0 %collective-permute-start = (f32[80,128]{1,0:T(8,128)S(1)}, f32[80,128]{1,0:T(8,128)S(1)}, u32[]{:S(2)}, u32[]{:S(2)}) collective-permute-start(f32[80,128]{1,0:T(8,128)S(1)} %get-tuple-element.51.refs_0_), channel_id=1, source_target_pairs={{0,28},{1,29},{2,30},{3,31},{4,24},{5,25},{6,26},{7,27},{8,20},{9,... | collective-permute-start | bytes 122888 | tf_op jit(solution)/shard_map/ppermute | solution.py:488
  5.8 4.6 %collective-permute-start.1 = (f32[80,128]{1,0:T(8,128)S(1)}, f32[80,128]{1,0:T(8,128)S(1)}, u32[]{:S(2)}, u32[]{:S(2)}) collective-permute-start(f32[80,128]{1,0:T(8,128)S(1)} %get-tuple-element.52.refs_1_), channel_id=1, source_target_pairs={{0,20},{1,21},{2,22},{3,23},{4,16},{5,17},{6,18},{7,19},{8,28},{9,... | collective-permute-start | bytes 122888 | tf_op jit(solution)/shard_map/ppermute | solution.py:488
  6.6 3.8 %collective-permute-start.2 = (f32[80,128]{1,0:T(8,128)S(1)}, f32[80,128]{1,0:T(8,128)S(1)}, u32[]{:S(2)}, u32[]{:S(2)}) collective-permute-start(f32[80,128]{1,0:T(8,128)S(1)} %get-tuple-element.53.refs_2_), channel_id=1, source_target_pairs={{0,12},{1,13},{2,14},{3,15},{4,8},{5,9},{6,10},{7,11},{8,4},{9,5},... | collective-permute-start | bytes 122888 | tf_op jit(solution)/shard_map/ppermute | solution.py:488
  10.4 1.3 %collective-permute-start.3 = (f32[160,128]{1,0:T(8,128)S(1)}, f32[160,128]{1,0:T(8,128)S(1)}, u32[]{:S(2)}, u32[]{:S(2)}) collective-permute-start(f32[160,128]{1,0:T(8,128)S(1)} %pad_maximum_fusion.1), channel_id=1, source_target_pairs={{0,4},{1,5},{2,6},{3,7},{4,0},{5,1},{6,2},{7,3},{8,12},{9,13},{10,... | collective-permute-start | bytes 245768 | tf_op jit(solution)/shard_map/ppermute | solution.py:488
  12.6 4.6 %collective-permute-start.4 = (f32[96,128]{1,0:T(8,128)S(1)}, f32[96,128]{1,0:T(8,128)S(1)}, u32[]{:S(2)}, u32[]{:S(2)}) collective-permute-start(f32[96,128]{1,0:T(8,128)S(1)} %get-tuple-element.64.refs_0_), channel_id=1, source_target_pairs={{0,28},{1,29},{2,30},{3,31},{4,24},{5,25},{6,26},{7,27},{8,20},{9,... | collective-permute-start | bytes 147464 | tf_op jit(solution)/shard_map/ppermute | solution.py:488
  14.5 3.8 %collective-permute-start.5 = (f32[96,128]{1,0:T(8,128)S(1)}, f32[96,128]{1,0:T(8,128)S(1)}, u32[]{:S(2)}, u32[]{:S(2)}) collective-permute-start(f32[96,128]{1,0:T(8,128)S(1)} %get-tuple-element.65.refs_1_), channel_id=1, source_target_pairs={{0,20},{1,21},{2,22},{3,23},{4,16},{5,17},{6,18},{7,19},{8,28},{9,... | collective-permute-start | bytes 147464 | tf_op jit(solution)/shard_map/ppermute | solution.py:488
  14.8 3.5 %collective-permute-start.6 = (f32[96,128]{1,0:T(8,128)S(1)}, f32[96,128]{1,0:T(8,128)S(1)}, u32[]{:S(2)}, u32[]{:S(2)}) collective-permute-start(f32[96,128]{1,0:T(8,128)S(1)} %get-tuple-element.66.refs_2_), channel_id=1, source_target_pairs={{0,12},{1,13},{2,14},{3,15},{4,8},{5,9},{6,10},{7,11},{8,4},{9,5},... | collective-permute-start | bytes 147464 | tf_op jit(solution)/shard_map/ppermute | solution.py:488
  18.3 1.4 %collective-permute-start.7 = (f32[192,128]{1,0:T(8,128)S(1)}, f32[192,128]{1,0:T(8,128)S(1)}, u32[]{:S(2)}, u32[]{:S(2)}) collective-permute-start(f32[192,128]{1,0:T(8,128)S(1)} %pad_maximum_fusion), channel_id=1, source_target_pairs={{0,4},{1,5},{2,6},{3,7},{4,0},{5,1},{6,2},{7,3},{8,12},{9,13},{10,... | collective-permute-start | bytes 294920 | tf_op jit(solution)/shard_map/ppermute | solution.py:488
  20.9 1.2 %collective-permute-start.8 = (f32[32,128]{1,0:T(8,128)S(1)}, f32[32,128]{1,0:T(8,128)S(1)}, u32[]{:S(2)}, u32[]{:S(2)}) collective-permute-start(f32[32,128]{1,0:T(8,128)S(1)} %get-tuple-element.72.refs_1_), channel_id=1, source_target_pairs={{0,4},{1,5},{2,6},{3,7},{4,0},{5,1},{6,2},{7,3},{8,12},{9,13},{10,... | collective-permute-start | bytes 49160 | tf_op jit(solution)/shard_map/ppermute | solution.py:488
  22.3 4.1 %collective-permute-start.9 = (f32[32,128]{1,0:T(8,128)S(1)}, f32[32,128]{1,0:T(8,128)S(1)}, u32[]{:S(2)}, u32[]{:S(2)}) collective-permute-start(f32[32,128]{1,0:T(8,128)S(1)} %get-tuple-element.73.refs_3_), channel_id=1, source_target_pairs={{0,28},{1,29},{2,30},{3,31},{4,24},{5,25},{6,26},{7,27},{8,20},{9,... | collective-permute-start | bytes 49160 | tf_op jit(solution)/shard_map/ppermute | solution.py:488
  24.3 3.2 %collective-permute-start.10 = (f32[32,128]{1,0:T(8,128)S(1)}, f32[32,128]{1,0:T(8,128)S(1)}, u32[]{:S(2)}, u32[]{:S(2)}) collective-permute-start(f32[32,128]{1,0:T(8,128)S(1)} %get-tuple-element.74), channel_id=1, source_target_pairs={{0,20},{1,21},{2,22},{3,23},{4,16},{5,17},{6,18},{7,19},{8,28},{9,... | collective-permute-start | bytes 49160 | tf_op jit(solution)/shard_map/ppermute | solution.py:488
  24.7 3.2 %collective-permute-start.11 = (f32[32,128]{1,0:T(8,128)S(1)}, f32[32,128]{1,0:T(8,128)S(1)}, u32[]{:S(2)}, u32[]{:S(2)}) collective-permute-start(f32[32,128]{1,0:T(8,128)S(1)} %get-tuple-element.75), channel_id=1, source_target_pairs={{0,12},{1,13},{2,14},{3,15},{4,8},{5,9},{6,10},{7,11},{8,4},{9,5},... | collective-permute-start | bytes 49160 | tf_op jit(solution)/shard_map/ppermute | solution.py:488
  28.0 5.0 %collective-permute-start.12 = (f32[32,128]{1,0:T(8,128)S(1)}, f32[32,128]{1,0:T(8,128)S(1)}, u32[]{:S(2)}, u32[]{:S(2)}) collective-permute-start(f32[32,128]{1,0:T(8,128)S(1)} %get-tuple-element.76.refs_3_), channel_id=1, source_target_pairs={{0,7},{1,6},{2,5},{3,4},{4,3},{5,2},{6,1},{7,0},{8,15},{9,14},{10,... | collective-permute-start | bytes 49160 | tf_op jit(solution)/shard_map/ppermute | solution.py:488
  31.4 4.1 %collective-permute-start.13 = (f32[32,128]{1,0:T(8,128)S(1)}, f32[32,128]{1,0:T(8,128)S(1)}, u32[]{:S(2)}, u32[]{:S(2)}) collective-permute-start(f32[32,128]{1,0:T(8,128)S(1)} %get-tuple-element.77), channel_id=1, source_target_pairs={{0,6},{1,7},{2,4},{3,5},{4,2},{5,3},{6,0},{7,1},{8,14},{9,15},{10,... | collective-permute-start | bytes 49160 | tf_op jit(solution)/shard_map/ppermute | solution.py:488
  31.4 4.1 %collective-permute-start.14 = (f32[32,128]{1,0:T(8,128)S(1)}, f32[32,128]{1,0:T(8,128)S(1)}, u32[]{:S(2)}, u32[]{:S(2)}) collective-permute-start(f32[32,128]{1,0:T(8,128)S(1)} %get-tuple-element.78), channel_id=1, source_target_pairs={{0,5},{1,4},{2,7},{3,6},{4,1},{5,0},{6,3},{7,2},{8,13},{9,12},{10,... | collective-permute-start | bytes 49160 | tf_op jit(solution)/shard_map/ppermute | solution.py:488
where the time goes:
time: 38.3 us; the launch traced here: 38.1 us
  starting transfers between devices  15.5 us (40%)
  Pallas kernels  12 us (31%)
  waiting for transfers between devices  9.77 us (26%)
  between operations  0.75 us (2%)
    ppermute x15, starting transfers between devices, permute(): lax.ppermute(values, ('sub', 'rep'), [(at, at ^ offset) for at in range(p...  15.5 us
    ppermute x15, waiting for transfers between devices, permute(): lax.ppermute(values, ('sub', 'rep'), [(at, at ^ offset) for at in range(p...  9.77 us
    pallas_call x1, Pallas kernels, fused_body(): call(ready_kernel, [((rows, 3 * per_peer), jnp.bfloat16), halves, halves,...  2.97 us
    pallas_call x1, Pallas kernels, fused_body(): call(final_kernel, [((loads, rows), f32), ((MODES * groups, loads), f32)]...  2.56 us
    pallas_call x1, Pallas kernels, fused_body(): call(place_kernel, [((rows, rows - 2 * per_peer), jnp.bfloat16), ((short,...  1.77 us
    pallas_call x1, Pallas kernels, fused_body(): call(middle_kernel, [tall, ((GROUP, rows), f32), packed, wide, ((GROUP, l...  1.3 us
    pallas_call x1, Pallas kernels, fused_body(): call(second_kernel, [tall, packed], [VMEM] * (10 + len(got)), 'second')  1.25 us
    pallas_call x1, Pallas kernels, fused_body(): call(first_kernel, [half, tall, *pairs(height)], [VMEM] * (5 + len(send))...  0.79 us
  transfers between devices with their start and end apart: 15, of which 11 were waited for; matrix products, arithmetic and copies ran while one was open for 0% of the time, Pallas kernels for 14%

commit v1 on v0

--- a/solution.py
+++ b/solution.py
@@ -64,7 +64,7 @@
 
 
 def handed(got_ref, height, backwards=False):
-    starts = list(range(height, got_ref.shape[0], height))
+    starts = list(range(height, got_ref.shape[0] - height + 1, height))
     starts = [0, *(starts[::-1] if backwards else starts)]
     return jnp.concatenate([got_ref[at : at + height] for at in starts], axis=1)
 
@@ -306,14 +306,19 @@
     slots_ref, placed_ref, basis_ref, half_jump_ref, half_second_ref, scale_ref, early_ref, sums_ref, got_ref,
     near_ref, *refs,
 ):
-    *sent_refs, jump_ref, terms_ref = refs
+    *sent_refs, jump_ref, terms_ref, chip_ref = refs
     coarse = terms_ref.shape[0] // 2
     loads = basis_ref.shape[0] - coarse
     jump = for_other(near_ref, sent_refs) - handed(got_ref, loads + coarse, backwards=True)
-    inverse = 1.0 / scale_ref[:1]
-    jump = jump * inverse[:, : jump.shape[1]]
-    second = (half_second_ref[...] + split_dot(jump, placed_ref[1], NT)) * inverse
-    jump = half_jump_ref[...] + split_dot(jump, slots_ref[1], NT)
+    lanes = chip_ref.shape[1]
+    chip = jnp.maximum(scale_ref[:1, :lanes], got_ref[got_ref.shape[0] - 1 :])
+    chip_ref[...] = jnp.broadcast_to(chip, chip_ref.shape)
+    inverse = 1.0 / chip
+    ratio = scale_ref[:1, :lanes] * inverse
+    wide_inverse, wide_ratio = (jnp.concatenate([line] * (basis_ref.shape[1] // lanes), axis=1) for line in (inverse, ratio))
+    jump = jump * wide_inverse[:, : jump.shape[1]]
+    second = (half_second_ref[...] * wide_ratio + split_dot(jump, placed_ref[1], NT)) * wide_inverse
+    jump = half_jump_ref[...] * wide_ratio + split_dot(jump, slots_ref[1], NT)
     jump_ref[...] = jump
     basis = basis_ref[...]
     residual, jump_loads, second_loads = basis[:loads], jump[:loads], second[:loads]
@@ -336,12 +341,24 @@
     diagonal = jnp.sum(jnp.where(lane == row, z_z, 0.0), axis=0, keepdims=True)
     sums = by_load([jump_loads * jump_loads, jump_loads * second_loads, residual * second_loads])
     scalars = (
-        jnp.concatenate([sums_ref[0:1], sums_ref[1:2], sums[0:1], sums[1:2]], axis=1),
-        jnp.concatenate([sums[2:3], diagonal[:, :loads], scale_ref[:1, : 2 * loads]], axis=1),
-    )
-    terms_ref[...] = pack(
-        early_ref[2 * coarse :] + by_mode, scalars, [early_ref[:coarse] + top, early_ref[coarse : 2 * coarse] + low]
-    )
+        jnp.concatenate([sums_ref[0:1], sums_ref[1:2] * ratio[:, :loads], sums[0:1], sums[1:2]], axis=1),
+        jnp.concatenate([sums[2:3], diagonal[:, :loads], chip[:, : 2 * loads]], axis=1),
+    )
+    blocks = [
+        early_ref[at * coarse : (at + 1) * coarse] * jnp.where(group == 3, ratio, 1.0) + block
+        for at, block in enumerate((top, low))
+    ]
+    by_mode = early_ref[2 * coarse :] * jnp.where(strip == 1, ratio, 1.0) + by_mode
+    terms_ref[...] = pack(by_mode, scalars, blocks)
+
+
+def chip_kernel(other_ref, own_ref, *sum_refs):
+    own = own_ref[...]
+    row = lax.broadcasted_iota(jnp.int32, own.shape, 0)
+    lane = lax.broadcasted_iota(jnp.int32, own.shape, 1)
+    total = jnp.where((row == own.shape[0] - 1) & (lane >= own.shape[1] // 2), own, own + other_ref[...])
+    for ref in sum_refs:
+        ref[...] = total
 
 
 def summed(refs, power):
@@ -492,20 +509,18 @@
     return [permute(pair, 2 * (len(pairs) - at) + 1) for at, pair in enumerate(pairs)]
 
 
-def to_core(near, *pairs):
-    return permute(jnp.concatenate([near, *(pair[near.shape[0] :] for pair in pairs)], axis=0), 1)
+def to_core(near, *pairs, extra=()):
+    return permute(jnp.concatenate([near, *(pair[near.shape[0] :] for pair in pairs), *extra], axis=0), 1)
 
 
 def last_parts(terms, powers):
     chips = [(offset + 1, 0) for offset in reversed(range(2, lax.axis_size("sub"), 2))]
     planes = [(1, offset) for offset in reversed(range(1, lax.axis_size("rep")))]
-    copies = [terms]
-    for offsets, following in (([(1, 0)], len(chips)), (chips, len(planes))):
-        parts = [permute(copy, *offset) for copy, offset in zip(copies, offsets)]
-        kernel = functools.partial(sum_kernel, len(parts) + 1)
-        copies = call(kernel, [(terms.shape, terms.dtype)] * following, [VMEM] * (len(parts) + 2), "sum")(
-            powers, *parts, copies[0]
-        )
+    shape = (terms.shape, terms.dtype)
+    copies = call(chip_kernel, [shape] * len(chips), [VMEM] * 2, "chip")(permute(terms, 1), terms)
+    parts = [permute(copy, *offset) for copy, offset in zip(copies, chips)]
+    kernel = functools.partial(sum_kernel, len(parts) + 1)
+    copies = call(kernel, [shape] * len(planes), [VMEM] * (len(parts) + 2), "sum")(powers, *parts, copies[0])
     return [*(permute(copy, *offset) for copy, offset in zip(copies, planes)), copies[0]]
 
 
@@ -571,11 +586,11 @@
         "middle",
         flops=4 * rows * rows * height,
     )(edge, slots, operator, straight_jump, handed_jump, image)
-    got_near = to_core(near, *got[::-1])
+    got_near = to_core(near, *got[::-1], extra=[scale[:, :per_peer]])
     half_jump, half_second = call(
         second_half_kernel, [tall, tall], [VMEM] * (5 + 2 * len(got)), "second_half", flops=4 * rows * rows * height
     )(slots, placed, scale, stay, back, *image_send, *got)
-    jump, terms = call(second_kernel, [tall, packed], [VMEM] * (10 + len(got)), "second")(
+    jump, terms, scale = call(second_kernel, [tall, packed, ((GROUP, 4 * loads), f32)], [VMEM] * (10 + len(got)), "second")(
         slots, placed, basis, half_jump, half_second, scale, terms, sums, got_near, near, *image_send
     )
     parts = last_parts(terms, powers)

time: 38.3 us -> 38.1 us (level)
  transfers between devices with their start and end apart: 15 -> 15, of which waited for: 11 -> 10; matrix products, arithmetic and copies ran while one was open for 0% -> 0% of each run, Pallas kernels for 14% -> 14%
where the time goes in v1:
time: 38.1 us; the launch traced here: 37.9 us
  starting transfers between devices  15.5 us (41%)
  Pallas kernels  11.9 us (31%)
  waiting for transfers between devices  9.72 us (26%)
  between operations  0.77 us (2%)
    ppermute x15, starting transfers between devices, permute(): lax.ppermute(values, ('sub', 'rep'), [(at, at ^ offset) for at in range(p...  15.5 us
    ppermute x15, waiting for transfers between devices, permute(): lax.ppermute(values, ('sub', 'rep'), [(at, at ^ offset) for at in range(p...  9.72 us
    pallas_call x1, Pallas kernels, fused_body(): call(ready_kernel, [((rows, 3 * per_peer), jnp.bfloat16), halves, halves,...  2.97 us
    pallas_call x1, Pallas kernels, fused_body(): call(final_kernel, [((loads, rows), f32), ((MODES * groups, loads), f32)]...  2.56 us
    pallas_call x1, Pallas kernels, fused_body(): call(place_kernel, [((rows, rows - 2 * per_peer), jnp.bfloat16), ((short,...  1.77 us
    pallas_call x1, Pallas kernels, fused_body(): call(middle_kernel, [tall, ((GROUP, rows), f32), packed, wide, ((GROUP, l...  1.3 us
    pallas_call x1, Pallas kernels, fused_body(): call(second_kernel, [tall, packed, ((GROUP, 4 * loads), f32)], [VMEM] * (...  1.25 us
    pallas_call x1, Pallas kernels, fused_body(): call(first_kernel, [half, tall, *pairs(height)], [VMEM] * (5 + len(send))...  0.79 us
  transfers between devices with their start and end apart: 15, of which 10 were waited for; matrix products, arithmetic and copies ran while one was open for 0% of the time, Pallas kernels for 14%

profile of v1, /device:TPU:0, one launch (start us, length us, event | category | flops | bytes accessed | tf_op | source)
XLA Modules:
  0.0 37.9 jit_solution(6469436556213425641)
XLA Ops:
  0.6 1.8 %place.1 = (bf16[1024,768]{1,0:T(8,128)(2,1)S(1)}, f32[40,1024]{1,0:T(8,128)S(1)}, bf16[1,1024,1024]{2,1,0:T(8,128)(2,1)S(1)}, s32[1,1024]{1,0:T(1,128)S(1)}, f3...) custom-call(s32[1,1024]{1,0:T(1,128)} %route_hbm.1, s32[1,32]{1,0:T(1,128)} %bitcast.4, ...), custom_call_target="tpu_custom_call" | custom-call | bytes 1048576 | tf_op jit(solution)/shard_map/place/pallas_call | solution.py:550
  2.4 3.4 %collective-permute-start = (f32[80,128]{1,0:T(8,128)S(1)}, f32[80,128]{1,0:T(8,128)S(1)}, u32[]{:S(2)}, u32[]{:S(2)}) collective-permute-start(f32[80,128]{1,0:T(8,128)S(1)} %get-tuple-element.52.refs_0_), channel_id=1, source_target_pairs={{0,28},{1,29},{2,30},{3,31},{4,24},{5,25},{6,26},{7,27},{8,20},{9,... | collective-permute-start | bytes 122888 | tf_op jit(solution)/shard_map/ppermute | solution.py:505
  5.8 0.8 %collective-permute-start.1 = (f32[80,128]{1,0:T(8,128)S(1)}, f32[80,128]{1,0:T(8,128)S(1)}, u32[]{:S(2)}, u32[]{:S(2)}) collective-permute-start(f32[80,128]{1,0:T(8,128)S(1)} %get-tuple-element.53.refs_1_), channel_id=1, source_target_pairs={{0,20},{1,21},{2,22},{3,23},{4,16},{5,17},{6,18},{7,19},{8,28},{9,... | collective-permute-start | bytes 122888 | tf_op jit(solution)/shard_map/ppermute | solution.py:505
  6.6 0.1 collective-permute-start.2
  6.7 3.0 %ready.1 = (bf16[1024,384]{1,0:T(8,128)(2,1)S(1)}, bf16[2,1024,512]{2,1,0:T(8,128)(2,1)S(1)}, bf16[2,1024,512]{2,1,0:T(8,128)(2,1)S(1)}, f32[40,128]{1,0:T(8,128...) custom-call(s32[1,1024]{1,0:T(1,128)S(1)} %get-tuple-element.43.route_ref, ...), custom_call_target="tpu_custom_call" | custom-call | flops 2147483648 | bytes 1048576 | tf_op jit(solution)/shard_map/ready/pallas_call | solution.py:565
  9.7 0.7 %collective-permute-done.2.refs_5_ = f32[80,128]{1,0:T(8,128)S(1)} collective-permute-done((f32[80,128]{1,0:T(8,128)S(1)}, f32[80,128]{1,0:T(8,128)S(1)}, u32[]{:S(2)}, u32[]{:S(2)}) %collective-permute-start.2) | collective-permute-done | bytes 40992 | tf_op jit(solution)/shard_map/ppermute | solution.py:505
  10.4 0.0 collective-permute-done.1.refs_4_
  10.4 0.0 collective-permute-done.refs_3_
  10.4 0.2 collective-permute-start.3
  10.6 0.4 %first_half.1 = (f32[48,512]{1,0:T(8,128)S(1)}, f32[48,1024]{1,0:T(8,128)S(1)}) custom-call(bf16[2,1024,512]{2,1,0:T(8,128)(2,1)S(1)} %get-tuple-element.49.placed_ref, f32[40,128]{1,0:T(8,128)S(1)} %get-tuple-element.50.stay_ref, f32[40,128]{1,0:T(8,128)S(1)} %get-tuple-element.51.back_ref, f32[80,128]{1,0:T(8,128)S(1)} %get-tuple-element.52.refs_0_, ...), custom_call_target="tpu_custom_call" | custom-call | flops 100663296 | bytes 1048576 | tf_op jit(solution)/shard_map/first_half/pallas_call | solution.py:574
  11.1 0.7 %collective-permute-done.3.got_ref = f32[160,128]{1,0:T(8,128)S(1)} collective-permute-done((f32[160,128]{1,0:T(8,128)S(1)}, f32[160,128]{1,0:T(8,128)S(1)}, u32[]{:S(2)}, u32[]{:S(2)}) %collective-permute-start.3) | collective-permute-done | bytes 81952 | tf_op jit(solution)/shard_map/ppermute | solution.py:505
  11.8 0.8 %first.1 = (f32[48,512]{1,0:T(8,128)S(1)}, f32[48,1024]{1,0:T(8,128)S(1)}, f32[96,128]{1,0:T(8,128)S(1)}, f32[96,128]{1,0:T(8,128)S(1)}, f32[96,128]{1,0:T(8,128)S(1)}) custom-call(bf16[1024,768]{1,0:T(8,128)(2,1)S(1)} %get-tuple-element.44.far_ref, bf16[2,1024,512]{2,1,0:T(8,128)(2,1)S(1)} %get-tuple-element.49.placed_ref, ...), custom_call_target="tpu_custom_call" | custom-call | bytes 1048576 | tf_op jit(solution)/shard_map/first/pallas_call | solution.py:577
  12.6 1.9 %collective-permute-start.4 = (f32[96,128]{1,0:T(8,128)S(1)}, f32[96,128]{1,0:T(8,128)S(1)}, u32[]{:S(2)}, u32[]{:S(2)}) collective-permute-start(f32[96,128]{1,0:T(8,128)S(1)} %get-tuple-element.65.refs_0_), channel_id=1, source_target_pairs={{0,28},{1,29},{2,30},{3,31},{4,24},{5,25},{6,26},{7,27},{8,20},{9,... | collective-permute-start | bytes 147464 | tf_op jit(solution)/shard_map/ppermute | solution.py:505
  14.5 0.3 collective-permute-start.5
  14.8 0.8 %collective-permute-start.6 = (f32[96,128]{1,0:T(8,128)S(1)}, f32[96,128]{1,0:T(8,128)S(1)}, u32[]{:S(2)}, u32[]{:S(2)}) collective-permute-start(f32[96,128]{1,0:T(8,128)S(1)} %get-tuple-element.67.refs_2_), channel_id=1, source_target_pairs={{0,12},{1,13},{2,14},{3,15},{4,8},{5,9},{6,10},{7,11},{8,4},{9,5},... | collective-permute-start | bytes 147464 | tf_op jit(solution)/shard_map/ppermute | solution.py:505
  15.6 1.3 %middle.1 = (f32[48,1024]{1,0:T(8,128)S(1)}, f32[8,1024]{1,0:T(8,128)S(1)}, f32[32,128]{1,0:T(8,128)S(1)}, f32[48,128]{1,0:T(8,128)S(1)}, f32[8,32]{1,0:T(8,128)...) custom-call(bf16[1024,384]{1,0:T(8,128)(2,1)S(1)} %get-tuple-element.47.edge_ref, ...), custom_call_target="tpu_custom_call" | custom-call | flops 201326592 | bytes 1048576 | tf_op jit(solution)/shard_map/middle/pallas_call | solution.py:582
  16.9 1.4 %collective-permute-done.6.refs_5_ = f32[96,128]{1,0:T(8,128)S(1)} collective-permute-done((f32[96,128]{1,0:T(8,128)S(1)}, f32[96,128]{1,0:T(8,128)S(1)}, u32[]{:S(2)}, u32[]{:S(2)}) %collective-permute-start.6) | collective-permute-done | bytes 49184 | tf_op jit(solution)/shard_map/ppermute | solution.py:505
  18.3 0.0 collective-permute-done.5.refs_4_
  18.3 0.0 collective-permute-done.4.refs_3_
  18.3 0.4 %collective-permute-start.7 = (f32[200,128]{1,0:T(8,128)S(1)}, f32[200,128]{1,0:T(8,128)S(1)}, u32[]{:S(2)}, u32[]{:S(2)}) collective-permute-start(f32[200,128]{1,0:T(8,128)S(1)} %constant_dynamic-update-slice_fusion), channel_id=1, source_target_pairs={{0,4},{1,5},{2,6},{3,7},{4,0},{5,1},{6,2},{7,3},{8,12},{9,13},{10,... | collective-permute-start | bytes 307208 | tf_op jit(solution)/shard_map/ppermute | solution.py:505
  18.7 0.7 %second_half.1 = (f32[48,1024]{1,0:T(8,128)S(1)}, f32[48,1024]{1,0:T(8,128)S(1)}) custom-call(bf16[2,1024,512]{2,1,0:T(8,128)(2,1)S(1)} %get-tuple-element.48.slots_ref, bf16[2,1024,512]{2,1,0:T(8,128)(2,1)S(1)} %get-tuple-element.49.placed_ref, f32[8,1024]{1,0:T(8,128)S(1)} %get-tuple-element.62.scale_ref, f32[48,128]{1,0:T(8,128)S(1)} %get-tuple-element.63.stay_ref, ...), custom_call_target="tpu_custom_call" | custom-call | flops 201326592 | bytes 1048576 | tf_op jit(solution)/shard_map/second_half/pallas_call | solution.py:590
  19.5 0.2 collective-permute-done.7.got_ref
  19.7 1.2 %second.1 = (f32[48,1024]{1,0:T(8,128)S(1)}, f32[32,128]{1,0:T(8,128)S(1)}, f32[8,128]{1,0:T(8,128)S(1)}) custom-call(bf16[2,1024,512]{2,1,0:T(8,128)(2,1)S(1)} %get-tuple-element.48.slots_ref, bf16[2,1024,512]{2,1,0:T(8,128)(2,1)S(1)} %get-tuple-element.49.placed_ref, f32[48,1024]{1,0:T(8,128)S(1)} %get-tuple-element.61.basis_ref.refs_4_, ...), custom_call_target="tpu_custom_call" | custom-call | bytes 1048576 | tf_op jit(solution)/shard_map/second/pallas_call | solution.py:593
  21.0 0.4 %collective-permute-start.8 = (f32[32,128]{1,0:T(8,128)S(1)}, f32[32,128]{1,0:T(8,128)S(1)}, u32[]{:S(2)}, u32[]{:S(2)}) collective-permute-start(f32[32,128]{1,0:T(8,128)S(1)} %get-tuple-element.73.own_ref), channel_id=1, source_target_pairs={{0,4},{1,5},{2,6},{3,7},{4,0},{5,1},{6,2},{7,3},{8,12},{9,13},{10,... | collective-permute-start | bytes 49160 | tf_op jit(solution)/shard_map/ppermute | solution.py:505
  21.4 0.8 %collective-permute-done.8.other_ref = f32[32,128]{1,0:T(8,128)S(1)} collective-permute-done((f32[32,128]{1,0:T(8,128)S(1)}, f32[32,128]{1,0:T(8,128)S(1)}, u32[]{:S(2)}, u32[]{:S(2)}) %collective-permute-start.8) | collective-permute-done | bytes 16416 | tf_op jit(solution)/shard_map/ppermute | solution.py:505
  22.2 2.0 %collective-permute-start.9 = (f32[32,128]{1,0:T(8,128)S(1)}, f32[32,128]{1,0:T(8,128)S(1)}, u32[]{:S(2)}, u32[]{:S(2)}) collective-permute-start(f32[32,128]{1,0:T(8,128)S(1)} %get-tuple-element.74.refs_3_), channel_id=1, source_target_pairs={{0,28},{1,29},{2,30},{3,31},{4,24},{5,25},{6,26},{7,27},{8,20},{9,... | collective-permute-start | bytes 49160 | tf_op jit(solution)/shard_map/ppermute | solution.py:505
  24.2 0.4 %collective-permute-start.10 = (f32[32,128]{1,0:T(8,128)S(1)}, f32[32,128]{1,0:T(8,128)S(1)}, u32[]{:S(2)}, u32[]{:S(2)}) collective-permute-start(f32[32,128]{1,0:T(8,128)S(1)} %get-tuple-element.75), channel_id=1, source_target_pairs={{0,20},{1,21},{2,22},{3,23},{4,16},{5,17},{6,18},{7,19},{8,28},{9,... | collective-permute-start | bytes 49160 | tf_op jit(solution)/shard_map/ppermute | solution.py:505
  24.6 0.8 %collective-permute-start.11 = (f32[32,128]{1,0:T(8,128)S(1)}, f32[32,128]{1,0:T(8,128)S(1)}, u32[]{:S(2)}, u32[]{:S(2)}) collective-permute-start(f32[32,128]{1,0:T(8,128)S(1)} %get-tuple-element.76), channel_id=1, source_target_pairs={{0,12},{1,13},{2,14},{3,15},{4,8},{5,9},{6,10},{7,11},{8,4},{9,5},... | collective-permute-start | bytes 49160 | tf_op jit(solution)/shard_map/ppermute | solution.py:505
  25.4 0.9 %collective-permute-done.9.refs_0_ = f32[32,128]{1,0:T(8,128)S(1)} collective-permute-done((f32[32,128]{1,0:T(8,128)S(1)}, f32[32,128]{1,0:T(8,128)S(1)}, u32[]{:S(2)}, u32[]{:S(2)}) %collective-permute-start.9) | collective-permute-done | bytes 16416 | tf_op jit(solution)/shard_map/ppermute | solution.py:505
  26.3 1.1 %collective-permute-done.10.refs_1_ = f32[32,128]{1,0:T(8,128)S(1)} collective-permute-done((f32[32,128]{1,0:T(8,128)S(1)}, f32[32,128]{1,0:T(8,128)S(1)}, u32[]{:S(2)}, u32[]{:S(2)}) %collective-permute-start.10) | collective-permute-done | bytes 16416 | tf_op jit(solution)/shard_map/ppermute | solution.py:505
  27.4 0.4 %collective-permute-done.11.refs_2_ = f32[32,128]{1,0:T(8,128)S(1)} collective-permute-done((f32[32,128]{1,0:T(8,128)S(1)}, f32[32,128]{1,0:T(8,128)S(1)}, u32[]{:S(2)}, u32[]{:S(2)}) %collective-permute-start.11) | collective-permute-done | bytes 16416 | tf_op jit(solution)/shard_map/ppermute | solution.py:505
  27.8 0.1 sum.1
  27.9 3.4 %collective-permute-start.12 = (f32[32,128]{1,0:T(8,128)S(1)}, f32[32,128]{1,0:T(8,128)S(1)}, u32[]{:S(2)}, u32[]{:S(2)}) collective-permute-start(f32[32,128]{1,0:T(8,128)S(1)} %get-tuple-element.77.refs_3_), channel_id=1, source_target_pairs={{0,7},{1,6},{2,5},{3,4},{4,3},{5,2},{6,1},{7,0},{8,15},{9,14},{10,... | collective-permute-start | bytes 49160 | tf_op jit(solution)/shard_map/ppermute | solution.py:505
  31.3 0.0 collective-permute-start.13
  31.3 0.6 %collective-permute-start.14 = (f32[32,128]{1,0:T(8,128)S(1)}, f32[32,128]{1,0:T(8,128)S(1)}, u32[]{:S(2)}, u32[]{:S(2)}) collective-permute-start(f32[32,128]{1,0:T(8,128)S(1)} %get-tuple-element.79), channel_id=1, source_target_pairs={{0,5},{1,4},{2,7},{3,6},{4,1},{5,0},{6,3},{7,2},{8,13},{9,12},{10,... | collective-permute-start | bytes 49160 | tf_op jit(solution)/shard_map/ppermute | solution.py:505
  31.9 1.0 %collective-permute-done.12.refs_0_ = f32[32,128]{1,0:T(8,128)S(1)} collective-permute-done((f32[32,128]{1,0:T(8,128)S(1)}, f32[32,128]{1,0:T(8,128)S(1)}, u32[]{:S(2)}, u32[]{:S(2)}) %collective-permute-start.12) | collective-permute-done | bytes 16416 | tf_op jit(solution)/shard_map/ppermute | solution.py:505
  32.9 2.5 %collective-permute-done.13.refs_1_ = f32[32,128]{1,0:T(8,128)S(1)} collective-permute-done((f32[32,128]{1,0:T(8,128)S(1)}, f32[32,128]{1,0:T(8,128)S(1)}, u32[]{:S(2)}, u32[]{:S(2)}) %collective-permute-start.13) | collective-permute-done | bytes 16416 | tf_op jit(solution)/shard_map/ppermute | solution.py:505
  35.4 0.0 collective-permute-done.14.refs_2_
  35.4 2.6 %final.1 = (f32[32,1024]{1,0:T(8,128)}, f32[12,32]{1,0:T(8,128)}) custom-call(f32[32,128]{1,0:T(8,128)S(1)} %get-tuple-element.60.powers_ref, f32[32,128]{1,0:T(8,128)S(1)} %collective-permute-done.12.refs_0_, f32[32,128]{1,0:T(8,128)S(1)} %collective-permute-done.13.refs_1_, f32[32,128]{1,0:T(8,128)S(1)} %collective-permute-done.14.refs_2_, ...), custom_call_target="tpu_custom_call" | custom-call | bytes 1048576 | tf_op jit(solution)/shard_map/final/pallas_call | solution.py:597
  (10 shorter events, 0.1 us)
Async XLA Ops:
  2.4 8.0 %collective-permute-start = (f32[80,128]{1,0:T(8,128)S(1)}, f32[80,128]{1,0:T(8,128)S(1)}, u32[]{:S(2)}, u32[]{:S(2)}) collective-permute-start(f32[80,128]{1,0:T(8,128)S(1)} %get-tuple-element.52.refs_0_), channel_id=1, source_target_pairs={{0,28},{1,29},{2,30},{3,31},{4,24},{5,25},{6,26},{7,27},{8,20},{9,... | collective-permute-start | bytes 122888 | tf_op jit(solution)/shard_map/ppermute | solution.py:505
  5.8 4.6 %collective-permute-start.1 = (f32[80,128]{1,0:T(8,128)S(1)}, f32[80,128]{1,0:T(8,128)S(1)}, u32[]{:S(2)}, u32[]{:S(2)}) collective-permute-start(f32[80,128]{1,0:T(8,128)S(1)} %get-tuple-element.53.refs_1_), channel_id=1, source_target_pairs={{0,20},{1,21},{2,22},{3,23},{4,16},{5,17},{6,18},{7,19},{8,28},{9,... | collective-permute-start | bytes 122888 | tf_op jit(solution)/shard_map/ppermute | solution.py:505
  6.6 3.8 %collective-permute-start.2 = (f32[80,128]{1,0:T(8,128)S(1)}, f32[80,128]{1,0:T(8,128)S(1)}, u32[]{:S(2)}, u32[]{:S(2)}) collective-permute-start(f32[80,128]{1,0:T(8,128)S(1)} %get-tuple-element.54.refs_2_), channel_id=1, source_target_pairs={{0,12},{1,13},{2,14},{3,15},{4,8},{5,9},{6,10},{7,11},{8,4},{9,5},... | collective-permute-start | bytes 122888 | tf_op jit(solution)/shard_map/ppermute | solution.py:505
  10.4 1.3 %collective-permute-start.3 = (f32[160,128]{1,0:T(8,128)S(1)}, f32[160,128]{1,0:T(8,128)S(1)}, u32[]{:S(2)}, u32[]{:S(2)}) collective-permute-start(f32[160,128]{1,0:T(8,128)S(1)} %pad_maximum_fusion), channel_id=1, source_target_pairs={{0,4},{1,5},{2,6},{3,7},{4,0},{5,1},{6,2},{7,3},{8,12},{9,13},{10,... | collective-permute-start | bytes 245768 | tf_op jit(solution)/shard_map/ppermute | solution.py:505
  12.6 5.7 %collective-permute-start.4 = (f32[96,128]{1,0:T(8,128)S(1)}, f32[96,128]{1,0:T(8,128)S(1)}, u32[]{:S(2)}, u32[]{:S(2)}) collective-permute-start(f32[96,128]{1,0:T(8,128)S(1)} %get-tuple-element.65.refs_0_), channel_id=1, source_target_pairs={{0,28},{1,29},{2,30},{3,31},{4,24},{5,25},{6,26},{7,27},{8,20},{9,... | collective-permute-start | bytes 147464 | tf_op jit(solution)/shard_map/ppermute | solution.py:505
  14.5 3.8 %collective-permute-start.5 = (f32[96,128]{1,0:T(8,128)S(1)}, f32[96,128]{1,0:T(8,128)S(1)}, u32[]{:S(2)}, u32[]{:S(2)}) collective-permute-start(f32[96,128]{1,0:T(8,128)S(1)} %get-tuple-element.66.refs_1_), channel_id=1, source_target_pairs={{0,20},{1,21},{2,22},{3,23},{4,16},{5,17},{6,18},{7,19},{8,28},{9,... | collective-permute-start | bytes 147464 | tf_op jit(solution)/shard_map/ppermute | solution.py:505
  14.8 3.5 %collective-permute-start.6 = (f32[96,128]{1,0:T(8,128)S(1)}, f32[96,128]{1,0:T(8,128)S(1)}, u32[]{:S(2)}, u32[]{:S(2)}) collective-permute-start(f32[96,128]{1,0:T(8,128)S(1)} %get-tuple-element.67.refs_2_), channel_id=1, source_target_pairs={{0,12},{1,13},{2,14},{3,15},{4,8},{5,9},{6,10},{7,11},{8,4},{9,5},... | collective-permute-start | bytes 147464 | tf_op jit(solution)/shard_map/ppermute | solution.py:505
  18.3 1.4 %collective-permute-start.7 = (f32[200,128]{1,0:T(8,128)S(1)}, f32[200,128]{1,0:T(8,128)S(1)}, u32[]{:S(2)}, u32[]{:S(2)}) collective-permute-start(f32[200,128]{1,0:T(8,128)S(1)} %constant_dynamic-update-slice_fusion), channel_id=1, source_target_pairs={{0,4},{1,5},{2,6},{3,7},{4,0},{5,1},{6,2},{7,3},{8,12},{9,13},{10,... | collective-permute-start | bytes 307208 | tf_op jit(solution)/shard_map/ppermute | solution.py:505
  21.0 1.3 %collective-permute-start.8 = (f32[32,128]{1,0:T(8,128)S(1)}, f32[32,128]{1,0:T(8,128)S(1)}, u32[]{:S(2)}, u32[]{:S(2)}) collective-permute-start(f32[32,128]{1,0:T(8,128)S(1)} %get-tuple-element.73.own_ref), channel_id=1, source_target_pairs={{0,4},{1,5},{2,6},{3,7},{4,0},{5,1},{6,2},{7,3},{8,12},{9,13},{10,... | collective-permute-start | bytes 49160 | tf_op jit(solution)/shard_map/ppermute | solution.py:505
  22.2 4.1 %collective-permute-start.9 = (f32[32,128]{1,0:T(8,128)S(1)}, f32[32,128]{1,0:T(8,128)S(1)}, u32[]{:S(2)}, u32[]{:S(2)}) collective-permute-start(f32[32,128]{1,0:T(8,128)S(1)} %get-tuple-element.74.refs_3_), channel_id=1, source_target_pairs={{0,28},{1,29},{2,30},{3,31},{4,24},{5,25},{6,26},{7,27},{8,20},{9,... | collective-permute-start | bytes 49160 | tf_op jit(solution)/shard_map/ppermute | solution.py:505
  24.2 3.2 %collective-permute-start.10 = (f32[32,128]{1,0:T(8,128)S(1)}, f32[32,128]{1,0:T(8,128)S(1)}, u32[]{:S(2)}, u32[]{:S(2)}) collective-permute-start(f32[32,128]{1,0:T(8,128)S(1)} %get-tuple-element.75), channel_id=1, source_target_pairs={{0,20},{1,21},{2,22},{3,23},{4,16},{5,17},{6,18},{7,19},{8,28},{9,... | collective-permute-start | bytes 49160 | tf_op jit(solution)/shard_map/ppermute | solution.py:505
  24.6 3.2 %collective-permute-start.11 = (f32[32,128]{1,0:T(8,128)S(1)}, f32[32,128]{1,0:T(8,128)S(1)}, u32[]{:S(2)}, u32[]{:S(2)}) collective-permute-start(f32[32,128]{1,0:T(8,128)S(1)} %get-tuple-element.76), channel_id=1, source_target_pairs={{0,12},{1,13},{2,14},{3,15},{4,8},{5,9},{6,10},{7,11},{8,4},{9,5},... | collective-permute-start | bytes 49160 | tf_op jit(solution)/shard_map/ppermute | solution.py:505
  27.9 5.0 %collective-permute-start.12 = (f32[32,128]{1,0:T(8,128)S(1)}, f32[32,128]{1,0:T(8,128)S(1)}, u32[]{:S(2)}, u32[]{:S(2)}) collective-permute-start(f32[32,128]{1,0:T(8,128)S(1)} %get-tuple-element.77.refs_3_), channel_id=1, source_target_pairs={{0,7},{1,6},{2,5},{3,4},{4,3},{5,2},{6,1},{7,0},{8,15},{9,14},{10,... | collective-permute-start | bytes 49160 | tf_op jit(solution)/shard_map/ppermute | solution.py:505
  31.3 4.1 %collective-permute-start.13 = (f32[32,128]{1,0:T(8,128)S(1)}, f32[32,128]{1,0:T(8,128)S(1)}, u32[]{:S(2)}, u32[]{:S(2)}) collective-permute-start(f32[32,128]{1,0:T(8,128)S(1)} %get-tuple-element.78), channel_id=1, source_target_pairs={{0,6},{1,7},{2,4},{3,5},{4,2},{5,3},{6,0},{7,1},{8,14},{9,15},{10,... | collective-permute-start | bytes 49160 | tf_op jit(solution)/shard_map/ppermute | solution.py:505
  31.3 4.1 %collective-permute-start.14 = (f32[32,128]{1,0:T(8,128)S(1)}, f32[32,128]{1,0:T(8,128)S(1)}, u32[]{:S(2)}, u32[]{:S(2)}) collective-permute-start(f32[32,128]{1,0:T(8,128)S(1)} %get-tuple-element.79), channel_id=1, source_target_pairs={{0,5},{1,4},{2,7},{3,6},{4,1},{5,0},{6,3},{7,2},{8,13},{9,12},{10,... | collective-permute-start | bytes 49160 | tf_op jit(solution)/shard_map/ppermute | solution.py:505

commit v2 on v1

--- a/solution.py
+++ b/solution.py
@@ -108,11 +108,13 @@
         peer = own_index ^ (peers - 1 - at)
         far_ref[:, at * per_peer : (at + 1) * per_peer] = one_hot(route_ref, peer, per_peer)
 
-    for copy in copies:
+    for copy in (copies[3], *copies[:3]):
         copy.start()
     own_index = lax.axis_index("sub")
     device = own_index * lax.axis_size("rep") + lax.axis_index("rep")
     copies[0].wait()
+    for copy in copies[4:]:
+        copy.start()
     for at in range(peers - 4):
         build(at)
     copies[1].wait()

time: 38.1 us -> 38.8 us (1.018)
  Pallas kernels: 11.9 us -> 12.5 us
    pallas_call x1, Pallas kernels: 1.77 us -> 2.41 us  [fused_body(): call(place_kernel, [((rows, rows - 2 * per_peer), jnp.bfloat16), ((short,...]
where the time goes in v2:
time: 38.8 us; the launch traced here: 38.6 us
  starting transfers between devices  15.5 us (40%)
  Pallas kernels  12.5 us (32%)
  waiting for transfers between devices  9.73 us (25%)
  between operations  0.76 us (2%)
    ppermute x15, starting transfers between devices, permute(): lax.ppermute(values, ('sub', 'rep'), [(at, at ^ offset) for at in range(p...  15.5 us
    ppermute x15, waiting for transfers between devices, permute(): lax.ppermute(values, ('sub', 'rep'), [(at, at ^ offset) for at in range(p...  9.73 us
    pallas_call x1, Pallas kernels, fused_body(): call(ready_kernel, [((rows, 3 * per_peer), jnp.bfloat16), halves, halves,...  2.97 us
    pallas_call x1, Pallas kernels, fused_body(): call(final_kernel, [((loads, rows), f32), ((MODES * groups, loads), f32)]...  2.56 us
    pallas_call x1, Pallas kernels, fused_body(): call(place_kernel, [((rows, rows - 2 * per_peer), jnp.bfloat16), ((short,...  2.41 us
    pallas_call x1, Pallas kernels, fused_body(): call(middle_kernel, [tall, ((GROUP, rows), f32), packed, wide, ((GROUP, l...  1.29 us
    pallas_call x1, Pallas kernels, fused_body(): call(second_kernel, [tall, packed, ((GROUP, 4 * loads), f32)], [VMEM] * (...  1.25 us
    pallas_call x1, Pallas kernels, fused_body(): call(first_kernel, [half, tall, *pairs(height)], [VMEM] * (5 + len(send))...  0.79 us
  transfers between devices with their start and end apart: 15, of which 10 were waited for; matrix products, arithmetic and copies ran while one was open for 0% of the time, Pallas kernels for 14%

profile of v2, /device:TPU:0, one launch (start us, length us, event | category | flops | bytes accessed | tf_op | source)
XLA Modules:
  0.0 38.6 jit_solution(10204509609930881081)
XLA Ops:
  0.6 2.4 %place.1 = (bf16[1024,768]{1,0:T(8,128)(2,1)S(1)}, f32[40,1024]{1,0:T(8,128)S(1)}, bf16[1,1024,1024]{2,1,0:T(8,128)(2,1)S(1)}, s32[1,1024]{1,0:T(1,128)S(1)}, f3...) custom-call(s32[1,1024]{1,0:T(1,128)} %route_hbm.1, s32[1,32]{1,0:T(1,128)} %bitcast.4, ...), custom_call_target="tpu_custom_call" | custom-call | bytes 1048576 | tf_op jit(solution)/shard_map/place/pallas_call | solution.py:552
  3.0 3.4 %collective-permute-start = (f32[80,128]{1,0:T(8,128)S(1)}, f32[80,128]{1,0:T(8,128)S(1)}, u32[]{:S(2)}, u32[]{:S(2)}) collective-permute-start(f32[80,128]{1,0:T(8,128)S(1)} %get-tuple-element.52.refs_0_), channel_id=1, source_target_pairs={{0,28},{1,29},{2,30},{3,31},{4,24},{5,25},{6,26},{7,27},{8,20},{9,... | collective-permute-start | bytes 122888 | tf_op jit(solution)/shard_map/ppermute | solution.py:507
  6.4 0.8 %collective-permute-start.1 = (f32[80,128]{1,0:T(8,128)S(1)}, f32[80,128]{1,0:T(8,128)S(1)}, u32[]{:S(2)}, u32[]{:S(2)}) collective-permute-start(f32[80,128]{1,0:T(8,128)S(1)} %get-tuple-element.53.refs_1_), channel_id=1, source_target_pairs={{0,20},{1,21},{2,22},{3,23},{4,16},{5,17},{6,18},{7,19},{8,28},{9,... | collective-permute-start | bytes 122888 | tf_op jit(solution)/shard_map/ppermute | solution.py:507
  7.2 0.1 collective-permute-start.2
  7.4 3.0 %ready.1 = (bf16[1024,384]{1,0:T(8,128)(2,1)S(1)}, bf16[2,1024,512]{2,1,0:T(8,128)(2,1)S(1)}, bf16[2,1024,512]{2,1,0:T(8,128)(2,1)S(1)}, f32[40,128]{1,0:T(8,128...) custom-call(s32[1,1024]{1,0:T(1,128)S(1)} %get-tuple-element.43.route_ref, ...), custom_call_target="tpu_custom_call" | custom-call | flops 2147483648 | bytes 1048576 | tf_op jit(solution)/shard_map/ready/pallas_call | solution.py:567
  10.3 0.7 %collective-permute-done.2.refs_5_ = f32[80,128]{1,0:T(8,128)S(1)} collective-permute-done((f32[80,128]{1,0:T(8,128)S(1)}, f32[80,128]{1,0:T(8,128)S(1)}, u32[]{:S(2)}, u32[]{:S(2)}) %collective-permute-start.2) | collective-permute-done | bytes 40992 | tf_op jit(solution)/shard_map/ppermute | solution.py:507
  11.0 0.0 collective-permute-done.1.refs_4_
  11.0 0.0 collective-permute-done.refs_3_
  11.1 0.2 collective-permute-start.3
  11.3 0.4 %first_half.1 = (f32[48,512]{1,0:T(8,128)S(1)}, f32[48,1024]{1,0:T(8,128)S(1)}) custom-call(bf16[2,1024,512]{2,1,0:T(8,128)(2,1)S(1)} %get-tuple-element.49.placed_ref, f32[40,128]{1,0:T(8,128)S(1)} %get-tuple-element.50.stay_ref, f32[40,128]{1,0:T(8,128)S(1)} %get-tuple-element.51.back_ref, f32[80,128]{1,0:T(8,128)S(1)} %get-tuple-element.52.refs_0_, ...), custom_call_target="tpu_custom_call" | custom-call | flops 100663296 | bytes 1048576 | tf_op jit(solution)/shard_map/first_half/pallas_call | solution.py:576
  11.7 0.7 %collective-permute-done.3.got_ref = f32[160,128]{1,0:T(8,128)S(1)} collective-permute-done((f32[160,128]{1,0:T(8,128)S(1)}, f32[160,128]{1,0:T(8,128)S(1)}, u32[]{:S(2)}, u32[]{:S(2)}) %collective-permute-start.3) | collective-permute-done | bytes 81952 | tf_op jit(solution)/shard_map/ppermute | solution.py:507
  12.4 0.8 %first.1 = (f32[48,512]{1,0:T(8,128)S(1)}, f32[48,1024]{1,0:T(8,128)S(1)}, f32[96,128]{1,0:T(8,128)S(1)}, f32[96,128]{1,0:T(8,128)S(1)}, f32[96,128]{1,0:T(8,128)S(1)}) custom-call(bf16[1024,768]{1,0:T(8,128)(2,1)S(1)} %get-tuple-element.44.far_ref, bf16[2,1024,512]{2,1,0:T(8,128)(2,1)S(1)} %get-tuple-element.49.placed_ref, ...), custom_call_target="tpu_custom_call" | custom-call | bytes 1048576 | tf_op jit(solution)/shard_map/first/pallas_call | solution.py:579
  13.2 1.9 %collective-permute-start.4 = (f32[96,128]{1,0:T(8,128)S(1)}, f32[96,128]{1,0:T(8,128)S(1)}, u32[]{:S(2)}, u32[]{:S(2)}) collective-permute-start(f32[96,128]{1,0:T(8,128)S(1)} %get-tuple-element.65.refs_0_), channel_id=1, source_target_pairs={{0,28},{1,29},{2,30},{3,31},{4,24},{5,25},{6,26},{7,27},{8,20},{9,... | collective-permute-start | bytes 147464 | tf_op jit(solution)/shard_map/ppermute | solution.py:507
  15.1 0.3 collective-permute-start.5
  15.4 0.8 %collective-permute-start.6 = (f32[96,128]{1,0:T(8,128)S(1)}, f32[96,128]{1,0:T(8,128)S(1)}, u32[]{:S(2)}, u32[]{:S(2)}) collective-permute-start(f32[96,128]{1,0:T(8,128)S(1)} %get-tuple-element.67.refs_2_), channel_id=1, source_target_pairs={{0,12},{1,13},{2,14},{3,15},{4,8},{5,9},{6,10},{7,11},{8,4},{9,5},... | collective-permute-start | bytes 147464 | tf_op jit(solution)/shard_map/ppermute | solution.py:507
  16.2 1.3 %middle.1 = (f32[48,1024]{1,0:T(8,128)S(1)}, f32[8,1024]{1,0:T(8,128)S(1)}, f32[32,128]{1,0:T(8,128)S(1)}, f32[48,128]{1,0:T(8,128)S(1)}, f32[8,32]{1,0:T(8,128)...) custom-call(bf16[1024,384]{1,0:T(8,128)(2,1)S(1)} %get-tuple-element.47.edge_ref, ...), custom_call_target="tpu_custom_call" | custom-call | flops 201326592 | bytes 1048576 | tf_op jit(solution)/shard_map/middle/pallas_call | solution.py:584
  17.5 1.4 %collective-permute-done.6.refs_5_ = f32[96,128]{1,0:T(8,128)S(1)} collective-permute-done((f32[96,128]{1,0:T(8,128)S(1)}, f32[96,128]{1,0:T(8,128)S(1)}, u32[]{:S(2)}, u32[]{:S(2)}) %collective-permute-start.6) | collective-permute-done | bytes 49184 | tf_op jit(solution)/shard_map/ppermute | solution.py:507
  18.9 0.0 collective-permute-done.5.refs_4_
  18.9 0.0 collective-permute-done.4.refs_3_
  19.0 0.4 %collective-permute-start.7 = (f32[200,128]{1,0:T(8,128)S(1)}, f32[200,128]{1,0:T(8,128)S(1)}, u32[]{:S(2)}, u32[]{:S(2)}) collective-permute-start(f32[200,128]{1,0:T(8,128)S(1)} %constant_dynamic-update-slice_fusion), channel_id=1, source_target_pairs={{0,4},{1,5},{2,6},{3,7},{4,0},{5,1},{6,2},{7,3},{8,12},{9,13},{10,... | collective-permute-start | bytes 307208 | tf_op jit(solution)/shard_map/ppermute | solution.py:507
  19.4 0.7 %second_half.1 = (f32[48,1024]{1,0:T(8,128)S(1)}, f32[48,1024]{1,0:T(8,128)S(1)}) custom-call(bf16[2,1024,512]{2,1,0:T(8,128)(2,1)S(1)} %get-tuple-element.48.slots_ref, bf16[2,1024,512]{2,1,0:T(8,128)(2,1)S(1)} %get-tuple-element.49.placed_ref, f32[8,1024]{1,0:T(8,128)S(1)} %get-tuple-element.62.scale_ref, f32[48,128]{1,0:T(8,128)S(1)} %get-tuple-element.63.stay_ref, ...), custom_call_target="tpu_custom_call" | custom-call | flops 201326592 | bytes 1048576 | tf_op jit(solution)/shard_map/second_half/pallas_call | solution.py:592
  20.1 0.2 collective-permute-done.7.got_ref
  20.3 1.2 %second.1 = (f32[48,1024]{1,0:T(8,128)S(1)}, f32[32,128]{1,0:T(8,128)S(1)}, f32[8,128]{1,0:T(8,128)S(1)}) custom-call(bf16[2,1024,512]{2,1,0:T(8,128)(2,1)S(1)} %get-tuple-element.48.slots_ref, bf16[2,1024,512]{2,1,0:T(8,128)(2,1)S(1)} %get-tuple-element.49.placed_ref, f32[48,1024]{1,0:T(8,128)S(1)} %get-tuple-element.61.basis_ref.refs_4_, ...), custom_call_target="tpu_custom_call" | custom-call | bytes 1048576 | tf_op jit(solution)/shard_map/second/pallas_call | solution.py:595
  21.6 0.4 %collective-permute-start.8 = (f32[32,128]{1,0:T(8,128)S(1)}, f32[32,128]{1,0:T(8,128)S(1)}, u32[]{:S(2)}, u32[]{:S(2)}) collective-permute-start(f32[32,128]{1,0:T(8,128)S(1)} %get-tuple-element.73.own_ref), channel_id=1, source_target_pairs={{0,4},{1,5},{2,6},{3,7},{4,0},{5,1},{6,2},{7,3},{8,12},{9,13},{10,... | collective-permute-start | bytes 49160 | tf_op jit(solution)/shard_map/ppermute | solution.py:507
  22.0 0.8 %collective-permute-done.8.other_ref = f32[32,128]{1,0:T(8,128)S(1)} collective-permute-done((f32[32,128]{1,0:T(8,128)S(1)}, f32[32,128]{1,0:T(8,128)S(1)}, u32[]{:S(2)}, u32[]{:S(2)}) %collective-permute-start.8) | collective-permute-done | bytes 16416 | tf_op jit(solution)/shard_map/ppermute | solution.py:507
  22.9 2.0 %collective-permute-start.9 = (f32[32,128]{1,0:T(8,128)S(1)}, f32[32,128]{1,0:T(8,128)S(1)}, u32[]{:S(2)}, u32[]{:S(2)}) collective-permute-start(f32[32,128]{1,0:T(8,128)S(1)} %get-tuple-element.74.refs_3_), channel_id=1, source_target_pairs={{0,28},{1,29},{2,30},{3,31},{4,24},{5,25},{6,26},{7,27},{8,20},{9,... | collective-permute-start | bytes 49160 | tf_op jit(solution)/shard_map/ppermute | solution.py:507
  24.9 0.4 %collective-permute-start.10 = (f32[32,128]{1,0:T(8,128)S(1)}, f32[32,128]{1,0:T(8,128)S(1)}, u32[]{:S(2)}, u32[]{:S(2)}) collective-permute-start(f32[32,128]{1,0:T(8,128)S(1)} %get-tuple-element.75), channel_id=1, source_target_pairs={{0,20},{1,21},{2,22},{3,23},{4,16},{5,17},{6,18},{7,19},{8,28},{9,... | collective-permute-start | bytes 49160 | tf_op jit(solution)/shard_map/ppermute | solution.py:507
  25.3 0.8 %collective-permute-start.11 = (f32[32,128]{1,0:T(8,128)S(1)}, f32[32,128]{1,0:T(8,128)S(1)}, u32[]{:S(2)}, u32[]{:S(2)}) collective-permute-start(f32[32,128]{1,0:T(8,128)S(1)} %get-tuple-element.76), channel_id=1, source_target_pairs={{0,12},{1,13},{2,14},{3,15},{4,8},{5,9},{6,10},{7,11},{8,4},{9,5},... | collective-permute-start | bytes 49160 | tf_op jit(solution)/shard_map/ppermute | solution.py:507
  26.0 0.9 %collective-permute-done.9.refs_0_ = f32[32,128]{1,0:T(8,128)S(1)} collective-permute-done((f32[32,128]{1,0:T(8,128)S(1)}, f32[32,128]{1,0:T(8,128)S(1)}, u32[]{:S(2)}, u32[]{:S(2)}) %collective-permute-start.9) | collective-permute-done | bytes 16416 | tf_op jit(solution)/shard_map/ppermute | solution.py:507
  26.9 1.1 %collective-permute-done.10.refs_1_ = f32[32,128]{1,0:T(8,128)S(1)} collective-permute-done((f32[32,128]{1,0:T(8,128)S(1)}, f32[32,128]{1,0:T(8,128)S(1)}, u32[]{:S(2)}, u32[]{:S(2)}) %collective-permute-start.10) | collective-permute-done | bytes 16416 | tf_op jit(solution)/shard_map/ppermute | solution.py:507
  28.0 0.4 %collective-permute-done.11.refs_2_ = f32[32,128]{1,0:T(8,128)S(1)} collective-permute-done((f32[32,128]{1,0:T(8,128)S(1)}, f32[32,128]{1,0:T(8,128)S(1)}, u32[]{:S(2)}, u32[]{:S(2)}) %collective-permute-start.11) | collective-permute-done | bytes 16416 | tf_op jit(solution)/shard_map/ppermute | solution.py:507
  28.4 0.1 sum.1
  28.5 3.4 %collective-permute-start.12 = (f32[32,128]{1,0:T(8,128)S(1)}, f32[32,128]{1,0:T(8,128)S(1)}, u32[]{:S(2)}, u32[]{:S(2)}) collective-permute-start(f32[32,128]{1,0:T(8,128)S(1)} %get-tuple-element.77.refs_3_), channel_id=1, source_target_pairs={{0,7},{1,6},{2,5},{3,4},{4,3},{5,2},{6,1},{7,0},{8,15},{9,14},{10,... | collective-permute-start | bytes 49160 | tf_op jit(solution)/shard_map/ppermute | solution.py:507
  32.0 0.0 collective-permute-start.13
  32.0 0.6 %collective-permute-start.14 = (f32[32,128]{1,0:T(8,128)S(1)}, f32[32,128]{1,0:T(8,128)S(1)}, u32[]{:S(2)}, u32[]{:S(2)}) collective-permute-start(f32[32,128]{1,0:T(8,128)S(1)} %get-tuple-element.79), channel_id=1, source_target_pairs={{0,5},{1,4},{2,7},{3,6},{4,1},{5,0},{6,3},{7,2},{8,13},{9,12},{10,... | collective-permute-start | bytes 49160 | tf_op jit(solution)/shard_map/ppermute | solution.py:507
  32.6 1.0 %collective-permute-done.12.refs_0_ = f32[32,128]{1,0:T(8,128)S(1)} collective-permute-done((f32[32,128]{1,0:T(8,128)S(1)}, f32[32,128]{1,0:T(8,128)S(1)}, u32[]{:S(2)}, u32[]{:S(2)}) %collective-permute-start.12) | collective-permute-done | bytes 16416 | tf_op jit(solution)/shard_map/ppermute | solution.py:507
  33.6 2.5 %collective-permute-done.13.refs_1_ = f32[32,128]{1,0:T(8,128)S(1)} collective-permute-done((f32[32,128]{1,0:T(8,128)S(1)}, f32[32,128]{1,0:T(8,128)S(1)}, u32[]{:S(2)}, u32[]{:S(2)}) %collective-permute-start.13) | collective-permute-done | bytes 16416 | tf_op jit(solution)/shard_map/ppermute | solution.py:507
  36.0 0.0 collective-permute-done.14.refs_2_
  36.0 2.6 %final.1 = (f32[32,1024]{1,0:T(8,128)}, f32[12,32]{1,0:T(8,128)}) custom-call(f32[32,128]{1,0:T(8,128)S(1)} %get-tuple-element.60.powers_ref, f32[32,128]{1,0:T(8,128)S(1)} %collective-permute-done.12.refs_0_, f32[32,128]{1,0:T(8,128)S(1)} %collective-permute-done.13.refs_1_, f32[32,128]{1,0:T(8,128)S(1)} %collective-permute-done.14.refs_2_, ...), custom_call_target="tpu_custom_call" | custom-call | bytes 1048576 | tf_op jit(solution)/shard_map/final/pallas_call | solution.py:599
  (10 shorter events, 0.1 us)
Async XLA Ops:
  3.0 8.0 %collective-permute-start = (f32[80,128]{1,0:T(8,128)S(1)}, f32[80,128]{1,0:T(8,128)S(1)}, u32[]{:S(2)}, u32[]{:S(2)}) collective-permute-start(f32[80,128]{1,0:T(8,128)S(1)} %get-tuple-element.52.refs_0_), channel_id=1, source_target_pairs={{0,28},{1,29},{2,30},{3,31},{4,24},{5,25},{6,26},{7,27},{8,20},{9,... | collective-permute-start | bytes 122888 | tf_op jit(solution)/shard_map/ppermute | solution.py:507
  6.4 4.6 %collective-permute-start.1 = (f32[80,128]{1,0:T(8,128)S(1)}, f32[80,128]{1,0:T(8,128)S(1)}, u32[]{:S(2)}, u32[]{:S(2)}) collective-permute-start(f32[80,128]{1,0:T(8,128)S(1)} %get-tuple-element.53.refs_1_), channel_id=1, source_target_pairs={{0,20},{1,21},{2,22},{3,23},{4,16},{5,17},{6,18},{7,19},{8,28},{9,... | collective-permute-start | bytes 122888 | tf_op jit(solution)/shard_map/ppermute | solution.py:507
  7.2 3.8 %collective-permute-start.2 = (f32[80,128]{1,0:T(8,128)S(1)}, f32[80,128]{1,0:T(8,128)S(1)}, u32[]{:S(2)}, u32[]{:S(2)}) collective-permute-start(f32[80,128]{1,0:T(8,128)S(1)} %get-tuple-element.54.refs_2_), channel_id=1, source_target_pairs={{0,12},{1,13},{2,14},{3,15},{4,8},{5,9},{6,10},{7,11},{8,4},{9,5},... | collective-permute-start | bytes 122888 | tf_op jit(solution)/shard_map/ppermute | solution.py:507
  11.1 1.3 %collective-permute-start.3 = (f32[160,128]{1,0:T(8,128)S(1)}, f32[160,128]{1,0:T(8,128)S(1)}, u32[]{:S(2)}, u32[]{:S(2)}) collective-permute-start(f32[160,128]{1,0:T(8,128)S(1)} %pad_maximum_fusion), channel_id=1, source_target_pairs={{0,4},{1,5},{2,6},{3,7},{4,0},{5,1},{6,2},{7,3},{8,12},{9,13},{10,... | collective-permute-start | bytes 245768 | tf_op jit(solution)/shard_map/ppermute | solution.py:507
  13.2 5.7 %collective-permute-start.4 = (f32[96,128]{1,0:T(8,128)S(1)}, f32[96,128]{1,0:T(8,128)S(1)}, u32[]{:S(2)}, u32[]{:S(2)}) collective-permute-start(f32[96,128]{1,0:T(8,128)S(1)} %get-tuple-element.65.refs_0_), channel_id=1, source_target_pairs={{0,28},{1,29},{2,30},{3,31},{4,24},{5,25},{6,26},{7,27},{8,20},{9,... | collective-permute-start | bytes 147464 | tf_op jit(solution)/shard_map/ppermute | solution.py:507
  15.1 3.8 %collective-permute-start.5 = (f32[96,128]{1,0:T(8,128)S(1)}, f32[96,128]{1,0:T(8,128)S(1)}, u32[]{:S(2)}, u32[]{:S(2)}) collective-permute-start(f32[96,128]{1,0:T(8,128)S(1)} %get-tuple-element.66.refs_1_), channel_id=1, source_target_pairs={{0,20},{1,21},{2,22},{3,23},{4,16},{5,17},{6,18},{7,19},{8,28},{9,... | collective-permute-start | bytes 147464 | tf_op jit(solution)/shard_map/ppermute | solution.py:507
  15.4 3.5 %collective-permute-start.6 = (f32[96,128]{1,0:T(8,128)S(1)}, f32[96,128]{1,0:T(8,128)S(1)}, u32[]{:S(2)}, u32[]{:S(2)}) collective-permute-start(f32[96,128]{1,0:T(8,128)S(1)} %get-tuple-element.67.refs_2_), channel_id=1, source_target_pairs={{0,12},{1,13},{2,14},{3,15},{4,8},{5,9},{6,10},{7,11},{8,4},{9,5},... | collective-permute-start | bytes 147464 | tf_op jit(solution)/shard_map/ppermute | solution.py:507
  19.0 1.4 %collective-permute-start.7 = (f32[200,128]{1,0:T(8,128)S(1)}, f32[200,128]{1,0:T(8,128)S(1)}, u32[]{:S(2)}, u32[]{:S(2)}) collective-permute-start(f32[200,128]{1,0:T(8,128)S(1)} %constant_dynamic-update-slice_fusion), channel_id=1, source_target_pairs={{0,4},{1,5},{2,6},{3,7},{4,0},{5,1},{6,2},{7,3},{8,12},{9,13},{10,... | collective-permute-start | bytes 307208 | tf_op jit(solution)/shard_map/ppermute | solution.py:507
  21.6 1.3 %collective-permute-start.8 = (f32[32,128]{1,0:T(8,128)S(1)}, f32[32,128]{1,0:T(8,128)S(1)}, u32[]{:S(2)}, u32[]{:S(2)}) collective-permute-start(f32[32,128]{1,0:T(8,128)S(1)} %get-tuple-element.73.own_ref), channel_id=1, source_target_pairs={{0,4},{1,5},{2,6},{3,7},{4,0},{5,1},{6,2},{7,3},{8,12},{9,13},{10,... | collective-permute-start | bytes 49160 | tf_op jit(solution)/shard_map/ppermute | solution.py:507
  22.9 4.1 %collective-permute-start.9 = (f32[32,128]{1,0:T(8,128)S(1)}, f32[32,128]{1,0:T(8,128)S(1)}, u32[]{:S(2)}, u32[]{:S(2)}) collective-permute-start(f32[32,128]{1,0:T(8,128)S(1)} %get-tuple-element.74.refs_3_), channel_id=1, source_target_pairs={{0,28},{1,29},{2,30},{3,31},{4,24},{5,25},{6,26},{7,27},{8,20},{9,... | collective-permute-start | bytes 49160 | tf_op jit(solution)/shard_map/ppermute | solution.py:507
  24.9 3.2 %collective-permute-start.10 = (f32[32,128]{1,0:T(8,128)S(1)}, f32[32,128]{1,0:T(8,128)S(1)}, u32[]{:S(2)}, u32[]{:S(2)}) collective-permute-start(f32[32,128]{1,0:T(8,128)S(1)} %get-tuple-element.75), channel_id=1, source_target_pairs={{0,20},{1,21},{2,22},{3,23},{4,16},{5,17},{6,18},{7,19},{8,28},{9,... | collective-permute-start | bytes 49160 | tf_op jit(solution)/shard_map/ppermute | solution.py:507
  25.3 3.2 %collective-permute-start.11 = (f32[32,128]{1,0:T(8,128)S(1)}, f32[32,128]{1,0:T(8,128)S(1)}, u32[]{:S(2)}, u32[]{:S(2)}) collective-permute-start(f32[32,128]{1,0:T(8,128)S(1)} %get-tuple-element.76), channel_id=1, source_target_pairs={{0,12},{1,13},{2,14},{3,15},{4,8},{5,9},{6,10},{7,11},{8,4},{9,5},... | collective-permute-start | bytes 49160 | tf_op jit(solution)/shard_map/ppermute | solution.py:507
  28.5 5.0 %collective-permute-start.12 = (f32[32,128]{1,0:T(8,128)S(1)}, f32[32,128]{1,0:T(8,128)S(1)}, u32[]{:S(2)}, u32[]{:S(2)}) collective-permute-start(f32[32,128]{1,0:T(8,128)S(1)} %get-tuple-element.77.refs_3_), channel_id=1, source_target_pairs={{0,7},{1,6},{2,5},{3,4},{4,3},{5,2},{6,1},{7,0},{8,15},{9,14},{10,... | collective-permute-start | bytes 49160 | tf_op jit(solution)/shard_map/ppermute | solution.py:507
  32.0 4.1 %collective-permute-start.13 = (f32[32,128]{1,0:T(8,128)S(1)}, f32[32,128]{1,0:T(8,128)S(1)}, u32[]{:S(2)}, u32[]{:S(2)}) collective-permute-start(f32[32,128]{1,0:T(8,128)S(1)} %get-tuple-element.78), channel_id=1, source_target_pairs={{0,6},{1,7},{2,4},{3,5},{4,2},{5,3},{6,0},{7,1},{8,14},{9,15},{10,... | collective-permute-start | bytes 49160 | tf_op jit(solution)/shard_map/ppermute | solution.py:507
  32.0 4.1 %collective-permute-start.14 = (f32[32,128]{1,0:T(8,128)S(1)}, f32[32,128]{1,0:T(8,128)S(1)}, u32[]{:S(2)}, u32[]{:S(2)}) collective-permute-start(f32[32,128]{1,0:T(8,128)S(1)} %get-tuple-element.79), channel_id=1, source_target_pairs={{0,5},{1,4},{2,7},{3,6},{4,1},{5,0},{6,3},{7,2},{8,13},{9,12},{10,... | collective-permute-start | bytes 49160 | tf_op jit(solution)/shard_map/ppermute | solution.py:507

commit v3 on v1

--- a/solution.py
+++ b/solution.py
@@ -108,7 +108,7 @@
         peer = own_index ^ (peers - 1 - at)
         far_ref[:, at * per_peer : (at + 1) * per_peer] = one_hot(route_ref, peer, per_peer)
 
-    for copy in copies:
+    for copy in (copies[0], *copies[4:], *copies[1:4]):
         copy.start()
     own_index = lax.axis_index("sub")
     device = own_index * lax.axis_size("rep") + lax.axis_index("rep")

time: 38.1 us -> 38.4 us (level)
  no operation moved by 1% of the time
where the time goes in v3:
time: 38.4 us; the launch traced here: 38.2 us
  starting transfers between devices  15.5 us (40%)
  Pallas kernels  12.2 us (32%)
  waiting for transfers between devices  9.72 us (25%)
  between operations  0.77 us (2%)
    ppermute x15, starting transfers between devices, permute(): lax.ppermute(values, ('sub', 'rep'), [(at, at ^ offset) for at in range(p...  15.5 us
    ppermute x15, waiting for transfers between devices, permute(): lax.ppermute(values, ('sub', 'rep'), [(at, at ^ offset) for at in range(p...  9.72 us
    pallas_call x1, Pallas kernels, fused_body(): call(ready_kernel, [((rows, 3 * per_peer), jnp.bfloat16), halves, halves,...  2.97 us
    pallas_call x1, Pallas kernels, fused_body(): call(final_kernel, [((loads, rows), f32), ((MODES * groups, loads), f32)]...  2.56 us
    pallas_call x1, Pallas kernels, fused_body(): call(place_kernel, [((rows, rows - 2 * per_peer), jnp.bfloat16), ((short,...  2.06 us
    pallas_call x1, Pallas kernels, fused_body(): call(middle_kernel, [tall, ((GROUP, rows), f32), packed, wide, ((GROUP, l...  1.3 us
    pallas_call x1, Pallas kernels, fused_body(): call(second_kernel, [tall, packed, ((GROUP, 4 * loads), f32)], [VMEM] * (...  1.25 us
    pallas_call x1, Pallas kernels, fused_body(): call(first_kernel, [half, tall, *pairs(height)], [VMEM] * (5 + len(send))...  0.79 us
  transfers between devices with their start and end apart: 15, of which 10 were waited for; matrix products, arithmetic and copies ran while one was open for 0% of the time, Pallas kernels for 14%

profile of v3, /device:TPU:0, one launch (start us, length us, event | category | flops | bytes accessed | tf_op | source)
XLA Modules:
  0.0 38.2 jit_solution(1679570503513244098)
XLA Ops:
  0.6 2.1 %place.1 = (bf16[1024,768]{1,0:T(8,128)(2,1)S(1)}, f32[40,1024]{1,0:T(8,128)S(1)}, bf16[1,1024,1024]{2,1,0:T(8,128)(2,1)S(1)}, s32[1,1024]{1,0:T(1,128)S(1)}, f3...) custom-call(s32[1,1024]{1,0:T(1,128)} %route_hbm.1, s32[1,32]{1,0:T(1,128)} %bitcast.4, ...), custom_call_target="tpu_custom_call" | custom-call | bytes 1048576 | tf_op jit(solution)/shard_map/place/pallas_call | solution.py:550
  2.7 3.4 %collective-permute-start = (f32[80,128]{1,0:T(8,128)S(1)}, f32[80,128]{1,0:T(8,128)S(1)}, u32[]{:S(2)}, u32[]{:S(2)}) collective-permute-start(f32[80,128]{1,0:T(8,128)S(1)} %get-tuple-element.52.refs_0_), channel_id=1, source_target_pairs={{0,28},{1,29},{2,30},{3,31},{4,24},{5,25},{6,26},{7,27},{8,20},{9,... | collective-permute-start | bytes 122888 | tf_op jit(solution)/shard_map/ppermute | solution.py:505
  6.1 0.8 %collective-permute-start.1 = (f32[80,128]{1,0:T(8,128)S(1)}, f32[80,128]{1,0:T(8,128)S(1)}, u32[]{:S(2)}, u32[]{:S(2)}) collective-permute-start(f32[80,128]{1,0:T(8,128)S(1)} %get-tuple-element.53.refs_1_), channel_id=1, source_target_pairs={{0,20},{1,21},{2,22},{3,23},{4,16},{5,17},{6,18},{7,19},{8,28},{9,... | collective-permute-start | bytes 122888 | tf_op jit(solution)/shard_map/ppermute | solution.py:505
  6.9 0.1 collective-permute-start.2
  7.0 3.0 %ready.1 = (bf16[1024,384]{1,0:T(8,128)(2,1)S(1)}, bf16[2,1024,512]{2,1,0:T(8,128)(2,1)S(1)}, bf16[2,1024,512]{2,1,0:T(8,128)(2,1)S(1)}, f32[40,128]{1,0:T(8,128...) custom-call(s32[1,1024]{1,0:T(1,128)S(1)} %get-tuple-element.43.route_ref, ...), custom_call_target="tpu_custom_call" | custom-call | flops 2147483648 | bytes 1048576 | tf_op jit(solution)/shard_map/ready/pallas_call | solution.py:565
  10.0 0.7 %collective-permute-done.2.refs_5_ = f32[80,128]{1,0:T(8,128)S(1)} collective-permute-done((f32[80,128]{1,0:T(8,128)S(1)}, f32[80,128]{1,0:T(8,128)S(1)}, u32[]{:S(2)}, u32[]{:S(2)}) %collective-permute-start.2) | collective-permute-done | bytes 40992 | tf_op jit(solution)/shard_map/ppermute | solution.py:505
  10.7 0.0 collective-permute-done.1.refs_4_
  10.7 0.0 collective-permute-done.refs_3_
  10.7 0.2 collective-permute-start.3
  10.9 0.4 %first_half.1 = (f32[48,512]{1,0:T(8,128)S(1)}, f32[48,1024]{1,0:T(8,128)S(1)}) custom-call(bf16[2,1024,512]{2,1,0:T(8,128)(2,1)S(1)} %get-tuple-element.49.placed_ref, f32[40,128]{1,0:T(8,128)S(1)} %get-tuple-element.50.stay_ref, f32[40,128]{1,0:T(8,128)S(1)} %get-tuple-element.51.back_ref, f32[80,128]{1,0:T(8,128)S(1)} %get-tuple-element.52.refs_0_, ...), custom_call_target="tpu_custom_call" | custom-call | flops 100663296 | bytes 1048576 | tf_op jit(solution)/shard_map/first_half/pallas_call | solution.py:574
  11.4 0.7 %collective-permute-done.3.got_ref = f32[160,128]{1,0:T(8,128)S(1)} collective-permute-done((f32[160,128]{1,0:T(8,128)S(1)}, f32[160,128]{1,0:T(8,128)S(1)}, u32[]{:S(2)}, u32[]{:S(2)}) %collective-permute-start.3) | collective-permute-done | bytes 81952 | tf_op jit(solution)/shard_map/ppermute | solution.py:505
  12.1 0.8 %first.1 = (f32[48,512]{1,0:T(8,128)S(1)}, f32[48,1024]{1,0:T(8,128)S(1)}, f32[96,128]{1,0:T(8,128)S(1)}, f32[96,128]{1,0:T(8,128)S(1)}, f32[96,128]{1,0:T(8,128)S(1)}) custom-call(bf16[1024,768]{1,0:T(8,128)(2,1)S(1)} %get-tuple-element.44.far_ref, bf16[2,1024,512]{2,1,0:T(8,128)(2,1)S(1)} %get-tuple-element.49.placed_ref, ...), custom_call_target="tpu_custom_call" | custom-call | bytes 1048576 | tf_op jit(solution)/shard_map/first/pallas_call | solution.py:577
  12.9 1.9 %collective-permute-start.4 = (f32[96,128]{1,0:T(8,128)S(1)}, f32[96,128]{1,0:T(8,128)S(1)}, u32[]{:S(2)}, u32[]{:S(2)}) collective-permute-start(f32[96,128]{1,0:T(8,128)S(1)} %get-tuple-element.65.refs_0_), channel_id=1, source_target_pairs={{0,28},{1,29},{2,30},{3,31},{4,24},{5,25},{6,26},{7,27},{8,20},{9,... | collective-permute-start | bytes 147464 | tf_op jit(solution)/shard_map/ppermute | solution.py:505
  14.8 0.3 collective-permute-start.5
  15.1 0.8 %collective-permute-start.6 = (f32[96,128]{1,0:T(8,128)S(1)}, f32[96,128]{1,0:T(8,128)S(1)}, u32[]{:S(2)}, u32[]{:S(2)}) collective-permute-start(f32[96,128]{1,0:T(8,128)S(1)} %get-tuple-element.67.refs_2_), channel_id=1, source_target_pairs={{0,12},{1,13},{2,14},{3,15},{4,8},{5,9},{6,10},{7,11},{8,4},{9,5},... | collective-permute-start | bytes 147464 | tf_op jit(solution)/shard_map/ppermute | solution.py:505
  15.8 1.3 %middle.1 = (f32[48,1024]{1,0:T(8,128)S(1)}, f32[8,1024]{1,0:T(8,128)S(1)}, f32[32,128]{1,0:T(8,128)S(1)}, f32[48,128]{1,0:T(8,128)S(1)}, f32[8,32]{1,0:T(8,128)...) custom-call(bf16[1024,384]{1,0:T(8,128)(2,1)S(1)} %get-tuple-element.47.edge_ref, ...), custom_call_target="tpu_custom_call" | custom-call | flops 201326592 | bytes 1048576 | tf_op jit(solution)/shard_map/middle/pallas_call | solution.py:582
  17.2 1.4 %collective-permute-done.6.refs_5_ = f32[96,128]{1,0:T(8,128)S(1)} collective-permute-done((f32[96,128]{1,0:T(8,128)S(1)}, f32[96,128]{1,0:T(8,128)S(1)}, u32[]{:S(2)}, u32[]{:S(2)}) %collective-permute-start.6) | collective-permute-done | bytes 49184 | tf_op jit(solution)/shard_map/ppermute | solution.py:505
  18.6 0.0 collective-permute-done.5.refs_4_
  18.6 0.0 collective-permute-done.4.refs_3_
  18.6 0.4 %collective-permute-start.7 = (f32[200,128]{1,0:T(8,128)S(1)}, f32[200,128]{1,0:T(8,128)S(1)}, u32[]{:S(2)}, u32[]{:S(2)}) collective-permute-start(f32[200,128]{1,0:T(8,128)S(1)} %constant_dynamic-update-slice_fusion), channel_id=1, source_target_pairs={{0,4},{1,5},{2,6},{3,7},{4,0},{5,1},{6,2},{7,3},{8,12},{9,13},{10,... | collective-permute-start | bytes 307208 | tf_op jit(solution)/shard_map/ppermute | solution.py:505
  19.0 0.7 %second_half.1 = (f32[48,1024]{1,0:T(8,128)S(1)}, f32[48,1024]{1,0:T(8,128)S(1)}) custom-call(bf16[2,1024,512]{2,1,0:T(8,128)(2,1)S(1)} %get-tuple-element.48.slots_ref, bf16[2,1024,512]{2,1,0:T(8,128)(2,1)S(1)} %get-tuple-element.49.placed_ref, f32[8,1024]{1,0:T(8,128)S(1)} %get-tuple-element.62.scale_ref, f32[48,128]{1,0:T(8,128)S(1)} %get-tuple-element.63.stay_ref, ...), custom_call_target="tpu_custom_call" | custom-call | flops 201326592 | bytes 1048576 | tf_op jit(solution)/shard_map/second_half/pallas_call | solution.py:590
  19.8 0.2 collective-permute-done.7.got_ref
  20.0 1.2 %second.1 = (f32[48,1024]{1,0:T(8,128)S(1)}, f32[32,128]{1,0:T(8,128)S(1)}, f32[8,128]{1,0:T(8,128)S(1)}) custom-call(bf16[2,1024,512]{2,1,0:T(8,128)(2,1)S(1)} %get-tuple-element.48.slots_ref, bf16[2,1024,512]{2,1,0:T(8,128)(2,1)S(1)} %get-tuple-element.49.placed_ref, f32[48,1024]{1,0:T(8,128)S(1)} %get-tuple-element.61.basis_ref.refs_4_, ...), custom_call_target="tpu_custom_call" | custom-call | bytes 1048576 | tf_op jit(solution)/shard_map/second/pallas_call | solution.py:593
  21.3 0.4 %collective-permute-start.8 = (f32[32,128]{1,0:T(8,128)S(1)}, f32[32,128]{1,0:T(8,128)S(1)}, u32[]{:S(2)}, u32[]{:S(2)}) collective-permute-start(f32[32,128]{1,0:T(8,128)S(1)} %get-tuple-element.73.own_ref), channel_id=1, source_target_pairs={{0,4},{1,5},{2,6},{3,7},{4,0},{5,1},{6,2},{7,3},{8,12},{9,13},{10,... | collective-permute-start | bytes 49160 | tf_op jit(solution)/shard_map/ppermute | solution.py:505
  21.7 0.8 %collective-permute-done.8.other_ref = f32[32,128]{1,0:T(8,128)S(1)} collective-permute-done((f32[32,128]{1,0:T(8,128)S(1)}, f32[32,128]{1,0:T(8,128)S(1)}, u32[]{:S(2)}, u32[]{:S(2)}) %collective-permute-start.8) | collective-permute-done | bytes 16416 | tf_op jit(solution)/shard_map/ppermute | solution.py:505
  22.5 2.1 %collective-permute-start.9 = (f32[32,128]{1,0:T(8,128)S(1)}, f32[32,128]{1,0:T(8,128)S(1)}, u32[]{:S(2)}, u32[]{:S(2)}) collective-permute-start(f32[32,128]{1,0:T(8,128)S(1)} %get-tuple-element.74.refs_3_), channel_id=1, source_target_pairs={{0,28},{1,29},{2,30},{3,31},{4,24},{5,25},{6,26},{7,27},{8,20},{9,... | collective-permute-start | bytes 49160 | tf_op jit(solution)/shard_map/ppermute | solution.py:505
  24.6 0.3 collective-permute-start.10
  24.9 0.8 %collective-permute-start.11 = (f32[32,128]{1,0:T(8,128)S(1)}, f32[32,128]{1,0:T(8,128)S(1)}, u32[]{:S(2)}, u32[]{:S(2)}) collective-permute-start(f32[32,128]{1,0:T(8,128)S(1)} %get-tuple-element.76), channel_id=1, source_target_pairs={{0,12},{1,13},{2,14},{3,15},{4,8},{5,9},{6,10},{7,11},{8,4},{9,5},... | collective-permute-start | bytes 49160 | tf_op jit(solution)/shard_map/ppermute | solution.py:505
  25.7 0.9 %collective-permute-done.9.refs_0_ = f32[32,128]{1,0:T(8,128)S(1)} collective-permute-done((f32[32,128]{1,0:T(8,128)S(1)}, f32[32,128]{1,0:T(8,128)S(1)}, u32[]{:S(2)}, u32[]{:S(2)}) %collective-permute-start.9) | collective-permute-done | bytes 16416 | tf_op jit(solution)/shard_map/ppermute | solution.py:505
  26.6 1.2 %collective-permute-done.10.refs_1_ = f32[32,128]{1,0:T(8,128)S(1)} collective-permute-done((f32[32,128]{1,0:T(8,128)S(1)}, f32[32,128]{1,0:T(8,128)S(1)}, u32[]{:S(2)}, u32[]{:S(2)}) %collective-permute-start.10) | collective-permute-done | bytes 16416 | tf_op jit(solution)/shard_map/ppermute | solution.py:505
  27.8 0.3 collective-permute-done.11.refs_2_
  28.1 0.1 sum.1
  28.2 3.4 %collective-permute-start.12 = (f32[32,128]{1,0:T(8,128)S(1)}, f32[32,128]{1,0:T(8,128)S(1)}, u32[]{:S(2)}, u32[]{:S(2)}) collective-permute-start(f32[32,128]{1,0:T(8,128)S(1)} %get-tuple-element.77.refs_3_), channel_id=1, source_target_pairs={{0,7},{1,6},{2,5},{3,4},{4,3},{5,2},{6,1},{7,0},{8,15},{9,14},{10,... | collective-permute-start | bytes 49160 | tf_op jit(solution)/shard_map/ppermute | solution.py:505
  31.6 0.0 collective-permute-start.13
  31.6 0.6 %collective-permute-start.14 = (f32[32,128]{1,0:T(8,128)S(1)}, f32[32,128]{1,0:T(8,128)S(1)}, u32[]{:S(2)}, u32[]{:S(2)}) collective-permute-start(f32[32,128]{1,0:T(8,128)S(1)} %get-tuple-element.79), channel_id=1, source_target_pairs={{0,5},{1,4},{2,7},{3,6},{4,1},{5,0},{6,3},{7,2},{8,13},{9,12},{10,... | collective-permute-start | bytes 49160 | tf_op jit(solution)/shard_map/ppermute | solution.py:505
  32.2 1.0 %collective-permute-done.12.refs_0_ = f32[32,128]{1,0:T(8,128)S(1)} collective-permute-done((f32[32,128]{1,0:T(8,128)S(1)}, f32[32,128]{1,0:T(8,128)S(1)}, u32[]{:S(2)}, u32[]{:S(2)}) %collective-permute-start.12) | collective-permute-done | bytes 16416 | tf_op jit(solution)/shard_map/ppermute | solution.py:505
  33.2 2.5 %collective-permute-done.13.refs_1_ = f32[32,128]{1,0:T(8,128)S(1)} collective-permute-done((f32[32,128]{1,0:T(8,128)S(1)}, f32[32,128]{1,0:T(8,128)S(1)}, u32[]{:S(2)}, u32[]{:S(2)}) %collective-permute-start.13) | collective-permute-done | bytes 16416 | tf_op jit(solution)/shard_map/ppermute | solution.py:505
  35.7 0.0 collective-permute-done.14.refs_2_
  35.7 2.6 %final.1 = (f32[32,1024]{1,0:T(8,128)}, f32[12,32]{1,0:T(8,128)}) custom-call(f32[32,128]{1,0:T(8,128)S(1)} %get-tuple-element.60.powers_ref, f32[32,128]{1,0:T(8,128)S(1)} %collective-permute-done.12.refs_0_, f32[32,128]{1,0:T(8,128)S(1)} %collective-permute-done.13.refs_1_, f32[32,128]{1,0:T(8,128)S(1)} %collective-permute-done.14.refs_2_, ...), custom_call_target="tpu_custom_call" | custom-call | bytes 1048576 | tf_op jit(solution)/shard_map/final/pallas_call | solution.py:597
  (10 shorter events, 0.1 us)
Async XLA Ops:
  2.7 8.0 %collective-permute-start = (f32[80,128]{1,0:T(8,128)S(1)}, f32[80,128]{1,0:T(8,128)S(1)}, u32[]{:S(2)}, u32[]{:S(2)}) collective-permute-start(f32[80,128]{1,0:T(8,128)S(1)} %get-tuple-element.52.refs_0_), channel_id=1, source_target_pairs={{0,28},{1,29},{2,30},{3,31},{4,24},{5,25},{6,26},{7,27},{8,20},{9,... | collective-permute-start | bytes 122888 | tf_op jit(solution)/shard_map/ppermute | solution.py:505
  6.1 4.6 %collective-permute-start.1 = (f32[80,128]{1,0:T(8,128)S(1)}, f32[80,128]{1,0:T(8,128)S(1)}, u32[]{:S(2)}, u32[]{:S(2)}) collective-permute-start(f32[80,128]{1,0:T(8,128)S(1)} %get-tuple-element.53.refs_1_), channel_id=1, source_target_pairs={{0,20},{1,21},{2,22},{3,23},{4,16},{5,17},{6,18},{7,19},{8,28},{9,... | collective-permute-start | bytes 122888 | tf_op jit(solution)/shard_map/ppermute | solution.py:505
  6.9 3.8 %collective-permute-start.2 = (f32[80,128]{1,0:T(8,128)S(1)}, f32[80,128]{1,0:T(8,128)S(1)}, u32[]{:S(2)}, u32[]{:S(2)}) collective-permute-start(f32[80,128]{1,0:T(8,128)S(1)} %get-tuple-element.54.refs_2_), channel_id=1, source_target_pairs={{0,12},{1,13},{2,14},{3,15},{4,8},{5,9},{6,10},{7,11},{8,4},{9,5},... | collective-permute-start | bytes 122888 | tf_op jit(solution)/shard_map/ppermute | solution.py:505
  10.7 1.3 %collective-permute-start.3 = (f32[160,128]{1,0:T(8,128)S(1)}, f32[160,128]{1,0:T(8,128)S(1)}, u32[]{:S(2)}, u32[]{:S(2)}) collective-permute-start(f32[160,128]{1,0:T(8,128)S(1)} %pad_maximum_fusion), channel_id=1, source_target_pairs={{0,4},{1,5},{2,6},{3,7},{4,0},{5,1},{6,2},{7,3},{8,12},{9,13},{10,... | collective-permute-start | bytes 245768 | tf_op jit(solution)/shard_map/ppermute | solution.py:505
  12.9 5.7 %collective-permute-start.4 = (f32[96,128]{1,0:T(8,128)S(1)}, f32[96,128]{1,0:T(8,128)S(1)}, u32[]{:S(2)}, u32[]{:S(2)}) collective-permute-start(f32[96,128]{1,0:T(8,128)S(1)} %get-tuple-element.65.refs_0_), channel_id=1, source_target_pairs={{0,28},{1,29},{2,30},{3,31},{4,24},{5,25},{6,26},{7,27},{8,20},{9,... | collective-permute-start | bytes 147464 | tf_op jit(solution)/shard_map/ppermute | solution.py:505
  14.8 3.8 %collective-permute-start.5 = (f32[96,128]{1,0:T(8,128)S(1)}, f32[96,128]{1,0:T(8,128)S(1)}, u32[]{:S(2)}, u32[]{:S(2)}) collective-permute-start(f32[96,128]{1,0:T(8,128)S(1)} %get-tuple-element.66.refs_1_), channel_id=1, source_target_pairs={{0,20},{1,21},{2,22},{3,23},{4,16},{5,17},{6,18},{7,19},{8,28},{9,... | collective-permute-start | bytes 147464 | tf_op jit(solution)/shard_map/ppermute | solution.py:505
  15.1 3.5 %collective-permute-start.6 = (f32[96,128]{1,0:T(8,128)S(1)}, f32[96,128]{1,0:T(8,128)S(1)}, u32[]{:S(2)}, u32[]{:S(2)}) collective-permute-start(f32[96,128]{1,0:T(8,128)S(1)} %get-tuple-element.67.refs_2_), channel_id=1, source_target_pairs={{0,12},{1,13},{2,14},{3,15},{4,8},{5,9},{6,10},{7,11},{8,4},{9,5},... | collective-permute-start | bytes 147464 | tf_op jit(solution)/shard_map/ppermute | solution.py:505
  18.6 1.4 %collective-permute-start.7 = (f32[200,128]{1,0:T(8,128)S(1)}, f32[200,128]{1,0:T(8,128)S(1)}, u32[]{:S(2)}, u32[]{:S(2)}) collective-permute-start(f32[200,128]{1,0:T(8,128)S(1)} %constant_dynamic-update-slice_fusion), channel_id=1, source_target_pairs={{0,4},{1,5},{2,6},{3,7},{4,0},{5,1},{6,2},{7,3},{8,12},{9,13},{10,... | collective-permute-start | bytes 307208 | tf_op jit(solution)/shard_map/ppermute | solution.py:505
  21.3 1.3 %collective-permute-start.8 = (f32[32,128]{1,0:T(8,128)S(1)}, f32[32,128]{1,0:T(8,128)S(1)}, u32[]{:S(2)}, u32[]{:S(2)}) collective-permute-start(f32[32,128]{1,0:T(8,128)S(1)} %get-tuple-element.73.own_ref), channel_id=1, source_target_pairs={{0,4},{1,5},{2,6},{3,7},{4,0},{5,1},{6,2},{7,3},{8,12},{9,13},{10,... | collective-permute-start | bytes 49160 | tf_op jit(solution)/shard_map/ppermute | solution.py:505
  22.5 4.1 %collective-permute-start.9 = (f32[32,128]{1,0:T(8,128)S(1)}, f32[32,128]{1,0:T(8,128)S(1)}, u32[]{:S(2)}, u32[]{:S(2)}) collective-permute-start(f32[32,128]{1,0:T(8,128)S(1)} %get-tuple-element.74.refs_3_), channel_id=1, source_target_pairs={{0,28},{1,29},{2,30},{3,31},{4,24},{5,25},{6,26},{7,27},{8,20},{9,... | collective-permute-start | bytes 49160 | tf_op jit(solution)/shard_map/ppermute | solution.py:505
  24.6 3.2 %collective-permute-start.10 = (f32[32,128]{1,0:T(8,128)S(1)}, f32[32,128]{1,0:T(8,128)S(1)}, u32[]{:S(2)}, u32[]{:S(2)}) collective-permute-start(f32[32,128]{1,0:T(8,128)S(1)} %get-tuple-element.75), channel_id=1, source_target_pairs={{0,20},{1,21},{2,22},{3,23},{4,16},{5,17},{6,18},{7,19},{8,28},{9,... | collective-permute-start | bytes 49160 | tf_op jit(solution)/shard_map/ppermute | solution.py:505
  24.9 3.2 %collective-permute-start.11 = (f32[32,128]{1,0:T(8,128)S(1)}, f32[32,128]{1,0:T(8,128)S(1)}, u32[]{:S(2)}, u32[]{:S(2)}) collective-permute-start(f32[32,128]{1,0:T(8,128)S(1)} %get-tuple-element.76), channel_id=1, source_target_pairs={{0,12},{1,13},{2,14},{3,15},{4,8},{5,9},{6,10},{7,11},{8,4},{9,5},... | collective-permute-start | bytes 49160 | tf_op jit(solution)/shard_map/ppermute | solution.py:505
  28.2 5.0 %collective-permute-start.12 = (f32[32,128]{1,0:T(8,128)S(1)}, f32[32,128]{1,0:T(8,128)S(1)}, u32[]{:S(2)}, u32[]{:S(2)}) collective-permute-start(f32[32,128]{1,0:T(8,128)S(1)} %get-tuple-element.77.refs_3_), channel_id=1, source_target_pairs={{0,7},{1,6},{2,5},{3,4},{4,3},{5,2},{6,1},{7,0},{8,15},{9,14},{10,... | collective-permute-start | bytes 49160 | tf_op jit(solution)/shard_map/ppermute | solution.py:505
  31.6 4.1 %collective-permute-start.13 = (f32[32,128]{1,0:T(8,128)S(1)}, f32[32,128]{1,0:T(8,128)S(1)}, u32[]{:S(2)}, u32[]{:S(2)}) collective-permute-start(f32[32,128]{1,0:T(8,128)S(1)} %get-tuple-element.78), channel_id=1, source_target_pairs={{0,6},{1,7},{2,4},{3,5},{4,2},{5,3},{6,0},{7,1},{8,14},{9,15},{10,... | collective-permute-start | bytes 49160 | tf_op jit(solution)/shard_map/ppermute | solution.py:505
  31.6 4.1 %collective-permute-start.14 = (f32[32,128]{1,0:T(8,128)S(1)}, f32[32,128]{1,0:T(8,128)S(1)}, u32[]{:S(2)}, u32[]{:S(2)}) collective-permute-start(f32[32,128]{1,0:T(8,128)S(1)} %get-tuple-element.79), channel_id=1, source_target_pairs={{0,5},{1,4},{2,7},{3,6},{4,1},{5,0},{6,3},{7,2},{8,13},{9,12},{10,... | collective-permute-start | bytes 49160 | tf_op jit(solution)/shard_map/ppermute | solution.py:505
